TPU v7x, 32 devices: a whole 2x2x4 slice. The times are simulated.
32 devices in a mesh: seq: 4 (over y, x), tp: 8 (over z, core).
Axes of the slice: x: 2, y: 2, z: 4, core: 2. Of those that a mesh axis runs over, the one named last changes fastest.
Arguments:
- query: bfloat16 [4096, 8192], P('seq', 'tp'), may hold values from -6 to 6
- key_in: bfloat16 [4096, 8192], P('seq', 'tp'), may hold values from -6 to 6
- value: bfloat16 [4096, 8192], P('seq', 'tp'), may hold values from -6 to 6
- gate: bfloat16 [4096, 8192], P('seq', 'tp'), may hold values from -8 to 8
- kv_start: float32 [64, 128, 128], P('tp'), may hold values from -240 to 240
- norm_gain: float32 [8192], P('tp'), may hold values from 0.5 to 2
- w_out: bfloat16 [8192, 6144], P('tp'), may hold values from -0.0625 to 0.0625
Outputs:
- mixed: bfloat16 [4096, 6144], P(('seq', 'tp'))
All inputs are finite; a program needn't handle non-finite values.
Results may differ from a plain program's by a relative error of at most 0.019.
Values may be sent and summed in bfloat16 or wider, within the bound.
A program may use at most 128 MiB of HBM per device.

v0:
```python
import jax
import jax.numpy as jnp
from jax import lax
from jax.sharding import PartitionSpec as P

HD = 128


def per_device(query, key_in, value, gate, kv_start, norm_gain, w_out):
    rows = query.shape[0]
    heads = query.shape[1] // HD
    block = min(512, rows)
    count = rows // block
    highest = lax.Precision.HIGHEST
    qa = (
        jax.nn.silu(query.astype(jnp.float32)).astype(jnp.bfloat16).reshape(count, block, heads, HD)
    )
    ka = (
        jax.nn.silu(key_in.astype(jnp.float32))
        .astype(jnp.bfloat16)
        .reshape(count, block, heads, HD)
    )
    va = value.reshape(count, block, heads, HD)
    block_states = jnp.einsum("nthd,nthe->nhde", ka, va, preferred_element_type=jnp.float32)
    own_total = jnp.sum(block_states, axis=0)
    local_before = jnp.cumsum(block_states, axis=0) - block_states
    gathered = lax.all_gather(
        own_total[None].astype(jnp.bfloat16), "seq", axis=0, tiled=True
    ).astype(jnp.float32)
    position = lax.axis_index("seq")
    below = (jnp.arange(gathered.shape[0]) < position).astype(jnp.float32)
    prior = jnp.sum(gathered * below[:, None, None, None], axis=0)
    states = local_before + (kv_start + prior)[None]
    q_float = qa.astype(jnp.float32)
    inter = jnp.einsum("nthd,nhde->nthe", q_float, states, precision=highest)
    scores = jnp.einsum("nthd,nshd->nhts", qa, ka, preferred_element_type=jnp.float32)
    causal = jnp.arange(block)[:, None] >= jnp.arange(block)[None, :]
    scores = jnp.where(causal[None, None], scores, jnp.float32(0.0))
    intra = jnp.einsum("nhts,nshe->nthe", scores, va.astype(jnp.float32), precision=highest)
    heads_out = (inter + intra).reshape(rows, heads, HD)
    scale = lax.rsqrt(jnp.mean(heads_out * heads_out, axis=-1, keepdims=True) + 1e-05)
    normed = (heads_out * scale).reshape(rows, heads * HD)
    attn = (normed * norm_gain[None, :] * jax.nn.sigmoid(gate.astype(jnp.float32))).astype(
        jnp.bfloat16
    )
    return lax.psum_scatter(
        jnp.dot(attn, w_out, preferred_element_type=jnp.float32).astype(jnp.bfloat16),
        "tp",
        scatter_dimension=0,
        tiled=True,
    )


def solution(mesh):
    in_specs = (
        P("seq", "tp"),
        P("seq", "tp"),
        P("seq", "tp"),
        P("seq", "tp"),
        P("tp", None, None),
        P("tp"),
        P("tp", None),
    )
    out_specs = P(("seq", "tp"), None)
    return jax.shard_map(
        per_device, mesh=mesh, in_specs=in_specs, out_specs=out_specs, check_vma=False
    )
```

profile of v0, /device:TPU:6, one launch (start us, length us, event | category | flops | bytes accessed | tf_op | source)
XLA Modules:
  0.0 227.0 jit_solution(14922868226787016128)
XLA Ops:
  6.5 0.0 all-gather.3.cloned.1.call-start
  6.5 2.8 %fusion.17 = bf16[128,8,8,128]{3,1,2,0:T(8,128)(2,1)S(1)} fusion(bf16[1024,1024]{1,0:T(8,128)(2,1)} %param.8), kind=kLoop, calls=%fused_computation.24 | loop fusion | flops 6291456 | bytes 4194304
  9.4 2.0 copy.37
  11.3 0.0 copy-done.4
  11.3 1.9 copy.38
  13.3 3.0 %copy.33 = bf16[2,512,8,128]{1,3,2,0:T(8,128)(2,1)S(1)} copy(bf16[2,512,8,128]{3,2,1,0:T(8,128)(2,1)} %bitcast.42) | data formatting | bytes 4194304 | tf_op jit(solution)/shard_map/reshape | solution.py:23
  16.3 3.2 %fusion.30 = (bf16[8,128,128]{2,1,0:T(8,128)(2,1)}, f32[2,8,128,128]{3,2,1,0:T(8,128)S(1)}) fusion(bf16[2,512,8,128]{1,3,2,0:T(8,128)(2,1)S(1)} %copy.33, bf16[2,512,8,128]{3,2,1,0:T(8,128)(2,1)} %bitcast.38), kind=kOutput, calls=%fused_computation.42 | convolution fusion | flops 268566528 | bytes 5505024 | tf_op jit(solution)/shard_map/nthd,nthe->nhde/dot_general | solution.py:24
  19.4 0.0 all-gather.3.cloned.1.call-update
  19.5 0.2 reduce-scatter.2.cloned.1.call-start
  19.7 0.0 copy-start
  19.7 2.8 %fusion.16 = bf16[128,8,8,128]{3,1,2,0:T(8,128)(2,1)S(1)} fusion(bf16[1024,1024]{1,0:T(8,128)(2,1)} %param.7), kind=kLoop, calls=%fused_computation.23 | loop fusion | flops 6291456 | bytes 4194304
  22.5 0.6 copy.39
  23.2 0.0 copy-start.1
  23.2 0.0 copy-done
  23.2 8.2 %fusion.23 = f32[2,8,512,512]{3,2,1,0:T(8,128)} fusion(bf16[2,512,8,128]{3,2,1,0:T(8,128)(2,1)S(1)} %bitcast.39, bf16[2,512,8,128]{3,2,1,0:T(8,128)(2,1)S(1)} %bitcast.40), kind=kOutput, calls=%fused_computation.31 | convolution fusion | flops 1073741824 | bytes 20971520 | tf_op jit(solution)/shard_map/nthd,nshd->nhts/dot_general | solution.py:36
  31.4 0.0 copy-done.1
  31.4 0.1 iota_compare_fusion
  31.4 18.3 %fusion = f32[2,8,512,128]{2,3,1,0:T(8,128)} fusion(bf16[2,512,8,128]{1,3,2,0:T(8,128)(2,1)S(1)} %copy.33, f32[2,8,512,512]{3,2,1,0:T(8,128)} %fusion.23, pred[512,512]{1,0:T(8,128)(4,1)S(1)} %iota_compare_fusion), kind=kOutput, calls=%fused_computation | convolution fusion | flops 6446645248 | bytes 23330816 | tf_op jit(solution)/shard_map/nhts,nshe->nthe/dot_general | solution.py:39
  49.8 1.7 fusion.18
  51.5 1.5 add.39
  53.0 0.3 fusion.27
  53.3 0.0 copy-done.2
  53.3 0.0 copy-done.3
  53.3 4.1 %multiply_reduce_fusion = (f32[2,512,8]{1,2,0:T(8,128)S(1)}, f32[2,512,8,128]{1,3,2,0:T(8,128)}) fusion(f32[2,8,512,128]{2,3,1,0:T(8,128)S(1)} %copy-done.3, f32[2,8,128,128]{3,2,1,0:T(8,128)S(1)} %fusion.27, bf16[2,512,8,128]{3,2,1,0:T(8,128)(2,1)S(1)} %bitcast.41), kind=kOutput, calls=%fused_computation.22 | convolution fusion | flops 1613750272 | bytes 11567104 | tf_op jit(solution)/shard_map/nthd,nhde->nthe/dot_general | solution.py:35
  57.5 0.2 copy.35
  57.7 5.3 %copy.34 = f32[2,512,8,128]{3,2,1,0:T(8,128)} copy(f32[2,512,8,128]{1,3,2,0:T(8,128)} %get-tuple-element.8) | data formatting | bytes 8388608 | tf_op jit(solution)/shard_map/add | solution.py:40
  63.0 2.5 %mul.46 = f32[1024,8,128]{2,1,0:T(8,128)} broadcast(f32[1024,8]{1,0:T(8,128)S(1)} %copy.35), dimensions={0,1} | broadcast | bytes 4227072 | tf_op jit(solution)/shard_map/mul | solution.py:42
  65.5 0.0 copy-done.5
  65.5 0.0 copy-done.6
  65.5 24.0 %convolution_convert_fusion = bf16[1024,6144]{1,0:T(8,128)(2,1)} fusion(bf16[1024,6144]{1,0:T(8,128)(2,1)} %param.13, f32[128,8,8,128]{3,2,1,0:T(8,128)} %bitcast.43, f32[128,8,8,128]{3,2,1,0:T(8,128)} %bitcast.44, bf16[1024,1024]{1,0:T(8,128)(2,1)S(1)} %copy-done.5, f32[1024]{0:T(1024)S(1)} %copy-done.6), kind=kOutput, calls=%fused_computation.2 | convolution fusion | flops 12899581952 | bytes 35655680 | tf_op jit(solution)/shard_map/dot_general | solution.py:47
  89.5 0.0 reduce-scatter.2.cloned.1.call-update
  89.5 130.6 %reduce-scatter.2.cloned.1.call-done = bf16[128,6144]{1,0:T(8,128)(2,1)} async-done(((bf16[1024,6144]{1,0:T(8,128)(2,1)}), bf16[128,6144]{1,0:T(8,128)(2,1)}) %reduce-scatter.2.cloned.1.call-update) | async-done | bytes 1572880 | tf_op jit(solution)/shard_map/reduce_scatter | solution.py:46
  (8 shorter events, 0.0 us)
Async XLA Ops:
  6.5 4.8 %copy-start.4 = (bf16[1024,1024]{1,0:T(8,128)(2,1)S(1)}, bf16[1024,1024]{1,0:T(8,128)(2,1)}, u32[]{:S(2)}) copy-start(bf16[1024,1024]{1,0:T(8,128)(2,1)} %param.9) | copy-start | bytes 6291460
  6.5 43.2 %all-gather.3.cloned.1.call-start = ((), (), s32[]{:S(2)}) async-start(), calls=%async_computation.2 | async-start | bytes 1310720 | tf_op jit(solution)/shard_map/all_gather | solution.py:27
  19.5 200.7 %reduce-scatter.2.cloned.1.call-start = ((), (), s32[]{:S(2)}) async-start(), calls=%async_computation.1 | async-start | bytes 14155776 | tf_op jit(solution)/shard_map/reduce_scatter | solution.py:46
  19.7 3.5 %copy-start = (bf16[128,8,8,128]{3,2,1,0:T(8,128)(2,1)S(1)}, bf16[128,8,8,128]{3,2,1,0:T(8,128)(2,1)}, u32[]{:S(2)}) copy-start(bf16[128,8,8,128]{3,2,1,0:T(8,128)(2,1)} %copy.37) | copy-start | bytes 6291460
  23.2 8.2 %copy-start.1 = (bf16[128,8,8,128]{3,2,1,0:T(8,128)(2,1)}, bf16[128,8,8,128]{3,2,1,0:T(8,128)(2,1)S(1)}, u32[]{:S(2)}) copy-start(bf16[128,8,8,128]{3,2,1,0:T(8,128)(2,1)S(1)} %copy.39) | copy-start | bytes 6291460
  49.8 3.5 %copy-start.2 = (bf16[128,8,8,128]{3,2,1,0:T(8,128)(2,1)S(1)}, bf16[128,8,8,128]{3,2,1,0:T(8,128)(2,1)}, u32[]{:S(2)}) copy-start(bf16[128,8,8,128]{3,2,1,0:T(8,128)(2,1)} %copy-done.1) | copy-start | bytes 6291460
  49.8 3.5 %copy-start.3 = (f32[2,8,512,128]{2,3,1,0:T(8,128)S(1)}, f32[2,8,512,128]{2,3,1,0:T(8,128)}, u32[]{:S(2)}) copy-start(f32[2,8,512,128]{2,3,1,0:T(8,128)} %fusion) | copy-start | bytes 12582916
  63.0 2.5 %copy-start.5 = (bf16[1024,1024]{1,0:T(8,128)(2,1)S(1)}, bf16[1024,1024]{1,0:T(8,128)(2,1)}, u32[]{:S(2)}) copy-start(bf16[1024,1024]{1,0:T(8,128)(2,1)} %param.10) | copy-start | bytes 6291460
  63.0 2.6 %copy-start.6 = (f32[1024]{0:T(1024)S(1)}, f32[1024]{0:T(1024)}, u32[]{:S(2)}) copy-start(f32[1024]{0:T(1024)} %param.12) | copy-start | bytes 12292
Sparse Core Ops, SparseCore 0:
  19.6 26.8 all-gather.2
  89.7 130.3 reduce-scatter.1
where the time goes:
time: 229 us; the launch traced here: 227 us
  waiting for transfers between devices  131 us (57%)
  matrix products  57.8 us (25%)
  local copies, waits for them, and re-layouts  15.6 us (7%)
  between operations  13.5 us (6%)
  other arithmetic  9.27 us (4%)
    reduce_scatter x1, waiting for transfers between devices, per_device(): lax.psum_scatter(jnp.dot(attn, w_out, preferred_element_type=jnp.float32)...  131 us
    dot_general x1, matrix products, per_device(): jnp.dot(attn, w_out, preferred_element_type=jnp.float32)  24 us
    dot_general x1, matrix products, per_device(): jnp.einsum('nhts,nshe->nthe', scores, va.astype(jnp.float32), precision=h...  18.3 us
    dot_general x1, matrix products, per_device(): jnp.einsum('nthd,nshd->nhts', qa, ka, preferred_element_type=jnp.float32)  8.18 us
    unnamed x2, other arithmetic  5.66 us
    add x1, local copies, waits for them, and re-layouts, per_device(): heads_out = (inter + intra).reshape(rows, heads, HD)  5.28 us
  transfers between devices with their start and end apart: 2, of which 1 were waited for; matrix products, arithmetic and copies ran while one was open for 13% of the time, Pallas kernels for 0%

commit v1 on v0

--- a/solution.py
+++ b/solution.py
@@ -1,12 +1,209 @@
+import functools
+
 import jax
 import jax.numpy as jnp
 from jax import lax
+from jax.experimental import pallas as pl
+from jax.experimental.pallas import tpu as pltpu
 from jax.sharding import PartitionSpec as P
 
 HD = 128
-
-
-def per_device(query, key_in, value, gate, kv_start, norm_gain, w_out):
+MESH = pl.DeviceIdType.MESH
+
+
+def other_chip(at):
+    return {"tp": at}
+
+
+def project_kernel(
+    chips, a_ref, w_hbm, o_ref, w_ref, pair_out, pair_in, line_out, from_low, from_high, acc,
+    w_sem, pair_out_sem, pair_in_sem, up_sem, low_sem, down_sem, high_sem,
+):
+    pieces, _, width = w_ref.shape
+    rows = o_ref.shape[0]
+    me = lax.axis_index("tp")
+    z, core = me // 2, me % 2
+    sibling = me + 1 - 2 * core
+    top = chips - 1
+
+    def weights(k):
+        return pltpu.make_async_copy(
+            w_hbm.at[:, pl.ds(pl.multiple_of(k * width, width), width)], w_ref.at[k], w_sem.at[k]
+        )
+
+    for k in range(pieces):
+        weights(k).start()
+
+    barrier = pltpu.get_barrier_semaphore()
+    pl.semaphore_signal(barrier, inc=1, device_id=other_chip(sibling), device_id_type=MESH)
+
+    @pl.when(z > 0)
+    def _():
+        pl.semaphore_signal(barrier, inc=1, device_id=other_chip(me - 2), device_id_type=MESH)
+
+    @pl.when(z < top)
+    def _():
+        pl.semaphore_signal(barrier, inc=1, device_id=other_chip(me + 2), device_id_type=MESH)
+
+    pl.semaphore_wait(barrier, 1 + jnp.minimum(z, 1) + jnp.minimum(top - z, 1))
+
+    def partial(d, side, k):
+        at = pl.multiple_of((2 * d + side) * rows, rows)
+        return jnp.dot(a_ref[pl.ds(at, rows), :], w_ref[k], preferred_element_type=jnp.float32)
+
+    def pair_copy(i):
+        return pltpu.make_async_remote_copy(
+            src_ref=pair_out.at[i], dst_ref=pair_in.at[i],
+            send_sem=pair_out_sem.at[i], recv_sem=pair_in_sem.at[i],
+            device_id=other_chip(sibling), device_id_type=MESH,
+        )
+
+    def up_copy(s):
+        return pltpu.make_async_remote_copy(
+            src_ref=line_out.at[(top - s // pieces) * pieces + s % pieces], dst_ref=from_low.at[s],
+            send_sem=up_sem.at[s], recv_sem=low_sem.at[s],
+            device_id=other_chip(me + 2), device_id_type=MESH,
+        )
+
+    def down_copy(s):
+        return pltpu.make_async_remote_copy(
+            src_ref=line_out.at[s], dst_ref=from_high.at[s],
+            send_sem=down_sem.at[s], recv_sem=high_sem.at[s],
+            device_id=other_chip(me - 2), device_id_type=MESH,
+        )
+
+    def chip_sum(d, k):
+        i = d * pieces + k
+        pair_out[i] = partial(d, 1 - core, k).astype(pair_out.dtype)
+        copy = pair_copy(i)
+        copy.start()
+        mine = partial(d, core, k)
+        copy.wait_recv()
+        return mine + pair_in[i].astype(jnp.float32)
+
+    def slot(s, carry):
+        k = s % pieces
+        turn = s // pieces
+
+        @pl.when(s < pieces)
+        def _():
+            weights(k).wait()
+
+        @pl.when(top - turn > z)
+        def _():
+            d = top - turn
+            i = d * pieces + k
+            total = chip_sum(d, k)
+
+            @pl.when(z > 0)
+            def _():
+                up_copy(s).wait_recv()
+                line_out[i] = (total + from_low[s].astype(jnp.float32)).astype(line_out.dtype)
+
+            @pl.when(z == 0)
+            def _():
+                line_out[i] = total.astype(line_out.dtype)
+
+            @pl.when(s >= 2)
+            def _():
+                up_copy(s - 2).wait_send()
+
+            up_copy(s).start()
+
+        @pl.when(turn < z)
+        def _():
+            total = chip_sum(turn, k)
+
+            @pl.when(z < top)
+            def _():
+                down_copy(s).wait_recv()
+                line_out[s] = (total + from_high[s].astype(jnp.float32)).astype(line_out.dtype)
+
+            @pl.when(z == top)
+            def _():
+                line_out[s] = total.astype(line_out.dtype)
+
+            @pl.when(s >= 2)
+            def _():
+                down_copy(s - 2).wait_send()
+
+            down_copy(s).start()
+
+        @pl.when(turn == 1)
+        def _():
+            acc[k] = chip_sum(z, k)
+
+        return carry
+
+    lax.fori_loop(0, top * pieces, slot, 0)
+
+    def finish(k, carry):
+        up_at = (top - z) * pieces + k
+        down_at = z * pieces + k
+
+        @pl.when(z < top)
+        def _():
+            down_copy(down_at).wait_recv()
+            acc[k] = acc[k] + from_high[down_at].astype(jnp.float32)
+
+        @pl.when(z > 0)
+        def _():
+            up_copy(up_at).wait_recv()
+            acc[k] = acc[k] + from_low[up_at].astype(jnp.float32)
+
+        o_ref[:, pl.ds(pl.multiple_of(k * width, width), width)] = acc[k].astype(o_ref.dtype)
+        return carry
+
+    lax.fori_loop(0, pieces, finish, 0)
+
+    for back in (2, 1):
+        @pl.when(z < top)
+        def _():
+            up_copy((top - z) * pieces - back).wait_send()
+
+        @pl.when(z > 0)
+        def _():
+            down_copy(z * pieces - back).wait_send()
+
+    def drain(i, carry):
+        pair_copy(i).wait_send()
+        return carry
+
+    lax.fori_loop(0, chips * pieces, drain, 0)
+
+
+def project(attn, w_out, n_tp):
+    depth, columns = w_out.shape
+    rows = attn.shape[0] // n_tp
+    chips = n_tp // 2
+    width = 1024
+    pieces = columns // width
+    every, passing = chips * pieces, (chips - 1) * pieces
+    chunk = lambda n: pltpu.VMEM((n, rows, width), jnp.bfloat16)
+    dma = lambda n: pltpu.SemaphoreType.DMA((n,))
+    return pl.pallas_call(
+        functools.partial(project_kernel, chips),
+        out_shape=jax.ShapeDtypeStruct((rows, columns), jnp.bfloat16),
+        in_specs=[pl.BlockSpec(memory_space=pltpu.VMEM), pl.BlockSpec(memory_space=pl.ANY)],
+        out_specs=pl.BlockSpec(memory_space=pltpu.VMEM),
+        scratch_shapes=[
+            pltpu.VMEM((pieces, depth, width), jnp.bfloat16),
+            chunk(every), chunk(every), chunk(every), chunk(passing), chunk(passing),
+            pltpu.VMEM((pieces, rows, width), jnp.float32),
+            dma(pieces), dma(every), dma(every),
+            dma(passing), dma(passing), dma(passing), dma(passing),
+        ],
+        compiler_params=pltpu.CompilerParams(
+            collective_id=0, has_side_effects=True, vmem_limit_bytes=60 * 2**20
+        ),
+        cost_estimate=pl.CostEstimate(
+            flops=2 * attn.shape[0] * depth * columns, bytes_accessed=2 * depth * columns,
+            transcendentals=0,
+        ),
+    )(attn, w_out)
+
+
+def per_device(n_tp, query, key_in, value, gate, kv_start, norm_gain, w_out):
     rows = query.shape[0]
     heads = query.shape[1] // HD
     block = min(512, rows)
@@ -43,12 +240,7 @@
     attn = (normed * norm_gain[None, :] * jax.nn.sigmoid(gate.astype(jnp.float32))).astype(
         jnp.bfloat16
     )
-    return lax.psum_scatter(
-        jnp.dot(attn, w_out, preferred_element_type=jnp.float32).astype(jnp.bfloat16),
-        "tp",
-        scatter_dimension=0,
-        tiled=True,
-    )
+    return project(attn, w_out, n_tp)
 
 
 def solution(mesh):
@@ -63,5 +255,5 @@
     )
     out_specs = P(("seq", "tp"), None)
     return jax.shard_map(
-        per_device, mesh=mesh, in_specs=in_specs, out_specs=out_specs, check_vma=False
-    )
+        functools.partial(per_device, mesh.shape["tp"]), mesh=mesh, in_specs=in_specs, out_specs=out_specs, check_vma=False
+    )

time: 229 us -> 250 us (1.092)
  the two profiles are of different devices: /device:TPU:6 before, /device:TPU:17 now
where the time goes in v1:
time: 250 us; the launch traced here: 249 us
  Pallas kernels  171 us (68%)
  matrix products  33.8 us (14%)
  local copies, waits for them, and re-layouts  18.2 us (7%)
  between operations  13.5 us (5%)
  other arithmetic  13 us (5%)
    pallas_call x1, Pallas kernels, project(): pl.pallas_call(functools.partial(project_kernel, chips), out_shape=jax.Sh...  171 us
    dot_general x1, matrix products, per_device(): jnp.einsum('nhts,nshe->nthe', scores, va.astype(jnp.float32), precision=h...  18.3 us
    unnamed x20, local copies, waits for them, and re-layouts  8.26 us
    dot_general x1, matrix products, per_device(): jnp.einsum('nthd,nshd->nhts', qa, ka, preferred_element_type=jnp.float32)  8.18 us
    unnamed x2, other arithmetic  5.66 us
    add x1, local copies, waits for them, and re-layouts, per_device(): heads_out = (inter + intra).reshape(rows, heads, HD)  5.4 us
  transfers between devices with their start and end apart: 1, of which 0 were waited for; matrix products, arithmetic and copies ran while one was open for 12% of the time, Pallas kernels for 0%

profile of v1, /device:TPU:17, one launch (start us, length us, event | category | flops | bytes accessed | tf_op | source)
XLA Modules:
  0.0 249.4 jit_solution(15000291116904600588)
XLA Ops:
  6.5 0.0 all-gather.3.cloned.1.call-start
  6.5 2.8 %fusion.16 = bf16[128,8,8,128]{3,1,2,0:T(8,128)(2,1)S(1)} fusion(bf16[1024,1024]{1,0:T(8,128)(2,1)} %param.8), kind=kLoop, calls=%fused_computation.23 | loop fusion | flops 6291456 | bytes 4194304
  9.4 2.0 copy.30
  11.3 0.0 copy-done.5
  11.3 1.9 copy.31
  13.3 3.2 %copy.26 = bf16[2,512,8,128]{1,3,2,0:T(8,128)(2,1)S(1)} copy(bf16[2,512,8,128]{3,2,1,0:T(8,128)(2,1)} %bitcast.41) | data formatting | bytes 4194304 | tf_op jit(solution)/shard_map/reshape | solution.py:220
  16.4 3.2 %fusion.26 = (bf16[8,128,128]{2,1,0:T(8,128)(2,1)}, f32[2,8,128,128]{3,2,1,0:T(8,128)S(1)}) fusion(bf16[2,512,8,128]{1,3,2,0:T(8,128)(2,1)S(1)} %copy.26, bf16[2,512,8,128]{3,2,1,0:T(8,128)(2,1)} %bitcast.35), kind=kOutput, calls=%fused_computation.38 | convolution fusion | flops 268566528 | bytes 5505024 | tf_op jit(solution)/shard_map/nthd,nthe->nhde/dot_general | solution.py:221
  19.6 0.0 all-gather.3.cloned.1.call-update
  19.6 0.0 copy-start
  19.6 2.8 %fusion.15 = bf16[128,8,8,128]{3,1,2,0:T(8,128)(2,1)S(1)} fusion(bf16[1024,1024]{1,0:T(8,128)(2,1)} %param.7), kind=kLoop, calls=%fused_computation.22 | loop fusion | flops 6291456 | bytes 4194304
  22.5 0.6 copy.32
  23.1 0.0 copy-start.1
  23.1 0.0 copy-done
  23.1 8.2 %fusion.20 = f32[2,8,512,512]{3,2,1,0:T(8,128)} fusion(bf16[2,512,8,128]{3,2,1,0:T(8,128)(2,1)S(1)} %bitcast.36, bf16[2,512,8,128]{3,2,1,0:T(8,128)(2,1)S(1)} %bitcast.37), kind=kOutput, calls=%fused_computation.28 | convolution fusion | flops 1073741824 | bytes 20971520 | tf_op jit(solution)/shard_map/nthd,nshd->nhts/dot_general | solution.py:233
  31.3 0.0 copy-done.1
  31.3 0.1 iota_compare_fusion
  31.4 18.3 %fusion = f32[2,8,512,128]{2,3,1,0:T(8,128)} fusion(bf16[2,512,8,128]{1,3,2,0:T(8,128)(2,1)S(1)} %copy.26, f32[2,8,512,512]{3,2,1,0:T(8,128)} %fusion.20, pred[512,512]{1,0:T(8,128)(4,1)S(1)} %iota_compare_fusion), kind=kOutput, calls=%fused_computation | convolution fusion | flops 6446645248 | bytes 23330816 | tf_op jit(solution)/shard_map/nhts,nshe->nthe/dot_general | solution.py:236
  49.7 1.7 fusion.17
  51.4 1.5 add.37
  53.0 0.3 fusion.24
  53.2 0.0 copy-done.2
  53.2 0.0 copy-done.4
  53.3 4.1 %multiply_reduce_fusion = (f32[2,512,8]{1,2,0:T(8,128)S(1)}, f32[2,512,8,128]{1,3,2,0:T(8,128)}) fusion(f32[2,8,512,128]{2,3,1,0:T(8,128)S(1)} %copy-done.4, f32[2,8,128,128]{3,2,1,0:T(8,128)S(1)} %fusion.24, bf16[2,512,8,128]{3,2,1,0:T(8,128)(2,1)S(1)} %bitcast.38), kind=kOutput, calls=%fused_computation.21 | convolution fusion | flops 1613750272 | bytes 11567104 | tf_op jit(solution)/shard_map/nthd,nhde->nthe/dot_general | solution.py:232
  57.4 0.2 copy.28
  57.6 0.0 copy-start.6
  57.6 5.4 %copy.27 = f32[2,512,8,128]{3,2,1,0:T(8,128)} copy(f32[2,512,8,128]{1,3,2,0:T(8,128)} %get-tuple-element.8) | data formatting | bytes 8388608 | tf_op jit(solution)/shard_map/add | solution.py:237
  63.0 1.1 mul.46
  64.2 0.0 copy-done.6
  64.2 1.0 copy-done.3
  65.2 3.7 %fusion.14.a_ref = bf16[1024,1024]{1,0:T(8,128)(2,1)} fusion(f32[128,8,8,128]{3,2,1,0:T(8,128)S(1)} %bitcast.40, f32[128,8,8,128]{3,2,1,0:T(8,128)S(1)} %bitcast.39, bf16[1024,1024]{1,0:T(8,128)(2,1)S(1)} %copy-done.6, f32[1024]{0:T(1024)S(1)} %copy-done.7), kind=kLoop, calls=%fused_computation.19 | loop fusion | flops 8388608 | bytes 12587008 | tf_op jit(solution)/shard_map/convert_element_type | solution.py:240
  68.9 170.9 %shard_map.73 = bf16[128,6144]{1,0:T(8,128)(2,1)} custom-call(bf16[1024,1024]{1,0:T(8,128)(2,1)} %fusion.14.a_ref, bf16[1024,6144]{1,0:T(8,128)(2,1)} %w_hbm.1), custom_call_target="tpu_custom_call" | custom-call | flops 12884901888 | bytes 12582912 | tf_op jit(solution)/shard_map/pallas_call | solution.py:184
  239.8 2.7 %copy.50 = bf16[128,6144]{1,0:T(8,128)(2,1)} copy(bf16[128,6144]{1,0:T(8,128)(2,1)} %shard_map.73) | data formatting | bytes 3145728
  (9 shorter events, 0.0 us)
Async XLA Ops:
  6.5 4.8 %copy-start.5 = (bf16[1024,1024]{1,0:T(8,128)(2,1)S(1)}, bf16[1024,1024]{1,0:T(8,128)(2,1)}, u32[]{:S(2)}) copy-start(bf16[1024,1024]{1,0:T(8,128)(2,1)} %param.9) | copy-start | bytes 6291460
  6.5 43.2 %all-gather.3.cloned.1.call-start = ((), (), s32[]{:S(2)}) async-start(), calls=%async_computation | async-start | bytes 1310720 | tf_op jit(solution)/shard_map/all_gather | solution.py:224
  19.6 3.5 %copy-start = (bf16[128,8,8,128]{3,2,1,0:T(8,128)(2,1)S(1)}, bf16[128,8,8,128]{3,2,1,0:T(8,128)(2,1)}, u32[]{:S(2)}) copy-start(bf16[128,8,8,128]{3,2,1,0:T(8,128)(2,1)} %copy.30) | copy-start | bytes 6291460
  23.1 8.2 %copy-start.1 = (bf16[128,8,8,128]{3,2,1,0:T(8,128)(2,1)}, bf16[128,8,8,128]{3,2,1,0:T(8,128)(2,1)S(1)}, u32[]{:S(2)}) copy-start(bf16[128,8,8,128]{3,2,1,0:T(8,128)(2,1)S(1)} %copy.32) | copy-start | bytes 6291460
  49.7 3.5 %copy-start.2 = (bf16[128,8,8,128]{3,2,1,0:T(8,128)(2,1)S(1)}, bf16[128,8,8,128]{3,2,1,0:T(8,128)(2,1)}, u32[]{:S(2)}) copy-start(bf16[128,8,8,128]{3,2,1,0:T(8,128)(2,1)} %copy-done.1) | copy-start | bytes 6291460
  49.7 3.5 %copy-start.4 = (f32[2,8,512,128]{2,3,1,0:T(8,128)S(1)}, f32[2,8,512,128]{2,3,1,0:T(8,128)}, u32[]{:S(2)}) copy-start(f32[2,8,512,128]{2,3,1,0:T(8,128)} %fusion) | copy-start | bytes 12582916
  57.6 6.6 %copy-start.6 = (bf16[1024,1024]{1,0:T(8,128)(2,1)S(1)}, bf16[1024,1024]{1,0:T(8,128)(2,1)}, u32[]{:S(2)}) copy-start(bf16[1024,1024]{1,0:T(8,128)(2,1)} %param.10) | copy-start | bytes 6291460
  63.0 2.2 copy-start.3
  63.0 2.2 copy-start.7
Sparse Core Ops, SparseCore 0:
  19.7 27.6 all-gather.2

commit v2 on v0

--- a/solution.py
+++ b/solution.py
@@ -1,12 +1,204 @@
+import functools
+
 import jax
 import jax.numpy as jnp
 from jax import lax
+from jax.experimental import pallas as pl
+from jax.experimental.pallas import tpu as pltpu
 from jax.sharding import PartitionSpec as P
 
 HD = 128
-
-
-def per_device(query, key_in, value, gate, kv_start, norm_gain, w_out):
+MESH = pl.DeviceIdType.MESH
+
+
+def project_kernel(
+    chips, a_ref, w_hbm, o_ref, w_ref, pair_out, pair_in, own, from_low, from_high, acc,
+    w_sem, pair_out_sem, pair_in_sem, up_sem, low_sem, down_sem, high_sem,
+):
+    pieces, depth, width = w_ref.shape
+    rows = o_ref.shape[0]
+    me = lax.axis_index("tp")
+    z, core = me // 2, me % 2
+    sibling = me + 1 - 2 * core
+    top = chips - 1
+
+    def weights(k):
+        return pltpu.make_async_copy(
+            w_hbm.at[:, pl.ds(pl.multiple_of(k * width, width), width)], w_ref.at[k], w_sem.at[k]
+        )
+
+    for k in range(pieces):
+        weights(k).start()
+
+    barrier = pltpu.get_barrier_semaphore()
+    pl.semaphore_signal(barrier, inc=1, device_id={"tp": sibling}, device_id_type=MESH)
+
+    @pl.when(z > 0)
+    def _():
+        pl.semaphore_signal(barrier, inc=1, device_id={"tp": me - 2}, device_id_type=MESH)
+
+    @pl.when(z < top)
+    def _():
+        pl.semaphore_signal(barrier, inc=1, device_id={"tp": me + 2}, device_id_type=MESH)
+
+    pl.semaphore_wait(barrier, 1 + jnp.minimum(z, 1) + jnp.minimum(top - z, 1))
+
+    def pair_copy(k):
+        return pltpu.make_async_remote_copy(
+            src_ref=pair_out.at[k], dst_ref=pair_in.at[k],
+            send_sem=pair_out_sem.at[k], recv_sem=pair_in_sem.at[k],
+            device_id={"tp": sibling}, device_id_type=MESH,
+        )
+
+    def up_copy(k, j):
+        return pltpu.make_async_remote_copy(
+            src_ref=own.at[k, top - j], dst_ref=from_low.at[k, j],
+            send_sem=up_sem.at[k, j], recv_sem=low_sem.at[k, j],
+            device_id={"tp": me + 2}, device_id_type=MESH,
+        )
+
+    def down_copy(k, j):
+        return pltpu.make_async_remote_copy(
+            src_ref=own.at[k, j], dst_ref=from_high.at[k, j],
+            send_sem=down_sem.at[k, j], recv_sem=high_sem.at[k, j],
+            device_id={"tp": me - 2}, device_id_type=MESH,
+        )
+
+    def partial(k, side):
+        a = a_ref[:, side].reshape(chips * rows, depth)
+        out = jnp.dot(a, w_ref[k], preferred_element_type=jnp.float32)
+        return out.astype(own.dtype).reshape(chips, rows, width)
+
+    def compute(k):
+        weights(k).wait()
+        pair_out[k] = partial(k, 1 - core)
+        pair_copy(k).start()
+        own[k] = partial(k, core)
+
+    def chip_sum(k, d):
+        return own[k, d].astype(jnp.float32) + pair_in[k, d].astype(jnp.float32)
+
+    def pass_on(k):
+        pair_copy(k).wait_recv()
+        for j in range(top):
+            up, down = top - j, j
+
+            @pl.when(up > z)
+            def _():
+                @pl.when(z > 0)
+                def _():
+                    up_copy(k, j).wait_recv()
+                    total = chip_sum(k, up) + from_low[k, j].astype(jnp.float32)
+                    own[k, up] = total.astype(own.dtype)
+
+                @pl.when(z == 0)
+                def _():
+                    own[k, up] = chip_sum(k, up).astype(own.dtype)
+
+                @pl.when(k >= 1)
+                def _():
+                    up_copy(k - 1, j).wait_send()
+
+                up_copy(k, j).start()
+
+            @pl.when(down < z)
+            def _():
+                @pl.when(z < top)
+                def _():
+                    down_copy(k, j).wait_recv()
+                    total = chip_sum(k, down) + from_high[k, j].astype(jnp.float32)
+                    own[k, down] = total.astype(own.dtype)
+
+                @pl.when(z == top)
+                def _():
+                    own[k, down] = chip_sum(k, down).astype(own.dtype)
+
+                @pl.when(k >= 1)
+                def _():
+                    down_copy(k - 1, j).wait_send()
+
+                down_copy(k, j).start()
+
+    def finish(k):
+        acc[...] = chip_sum(k, z)
+
+        @pl.when(z < top)
+        def _():
+            down_copy(k, z).wait_recv()
+            acc[...] = acc[...] + from_high[k, z].astype(jnp.float32)
+
+        @pl.when(z > 0)
+        def _():
+            up_copy(k, top - z).wait_recv()
+            acc[...] = acc[...] + from_low[k, top - z].astype(jnp.float32)
+
+        o_ref[:, pl.ds(pl.multiple_of(k * width, width), width)] = acc[...].astype(o_ref.dtype)
+
+    def step(k, carry):
+        @pl.when(k < pieces)
+        def _():
+            compute(k)
+
+        @pl.when((k >= 1) & (k <= pieces))
+        def _():
+            pass_on(k - 1)
+
+        @pl.when(k >= 2)
+        def _():
+            finish(k - 2)
+
+        return carry
+
+    lax.fori_loop(0, pieces + 2, step, 0)
+
+    for j in range(top):
+        @pl.when(top - j > z)
+        def _():
+            up_copy(pieces - 1, j).wait_send()
+
+        @pl.when(j < z)
+        def _():
+            down_copy(pieces - 1, j).wait_send()
+
+    def drain(k, carry):
+        pair_copy(k).wait_send()
+        return carry
+
+    lax.fori_loop(0, pieces, drain, 0)
+
+
+def project(attn, w_out, n_tp):
+    depth, columns = w_out.shape
+    rows = attn.shape[0] // n_tp
+    chips = n_tp // 2
+    width = 512
+    pieces = columns // width
+    chunk = lambda n: pltpu.VMEM((pieces, n, rows, width), jnp.bfloat16)
+    dma = lambda *n: pltpu.SemaphoreType.DMA(n)
+    return pl.pallas_call(
+        functools.partial(project_kernel, chips),
+        out_shape=jax.ShapeDtypeStruct((rows, columns), jnp.bfloat16),
+        in_specs=[pl.BlockSpec(memory_space=pltpu.VMEM), pl.BlockSpec(memory_space=pl.ANY)],
+        out_specs=pl.BlockSpec(memory_space=pltpu.VMEM),
+        scratch_shapes=[
+            pltpu.VMEM((pieces, depth, width), jnp.bfloat16),
+            chunk(chips), chunk(chips), chunk(chips), chunk(chips - 1), chunk(chips - 1),
+            pltpu.VMEM((rows, width), jnp.float32),
+            dma(pieces), dma(pieces), dma(pieces),
+            dma(pieces, chips - 1), dma(pieces, chips - 1),
+            dma(pieces, chips - 1), dma(pieces, chips - 1),
+        ],
+        compiler_params=pltpu.CompilerParams(
+            collective_id=0, has_side_effects=True, vmem_limit_bytes=60 * 2**20
+        ),
+        cost_estimate=pl.CostEstimate(
+            flops=2 * attn.shape[0] * depth * columns, bytes_accessed=2 * depth * columns,
+            transcendentals=0,
+        ),
+    )(attn.reshape(chips, 2, rows, depth), w_out)
+
+
+def per_device(n_tp, query, key_in, value, gate, kv_start, norm_gain, w_out):
     rows = query.shape[0]
     heads = query.shape[1] // HD
     block = min(512, rows)
@@ -43,12 +235,7 @@
     attn = (normed * norm_gain[None, :] * jax.nn.sigmoid(gate.astype(jnp.float32))).astype(
         jnp.bfloat16
     )
-    return lax.psum_scatter(
-        jnp.dot(attn, w_out, preferred_element_type=jnp.float32).astype(jnp.bfloat16),
-        "tp",
-        scatter_dimension=0,
-        tiled=True,
-    )
+    return project(attn, w_out, n_tp)
 
 
 def solution(mesh):
@@ -63,5 +250,5 @@
     )
     out_specs = P(("seq", "tp"), None)
     return jax.shard_map(
-        per_device, mesh=mesh, in_specs=in_specs, out_specs=out_specs, check_vma=False
-    )
+        functools.partial(per_device, mesh.shape["tp"]), mesh=mesh, in_specs=in_specs, out_specs=out_specs, check_vma=False
+    )

time: 229 us -> 221 us (0.965)
  Pallas kernels: 0 us -> 141 us
  waiting for transfers between devices: 131 us -> 0.02 us
  matrix products: 57.8 us -> 33.8 us
  other arithmetic: 9.27 us -> 13 us
  local copies, waits for them, and re-layouts: 15.6 us -> 18.2 us
    pallas_call x0 -> x1, Pallas kernels: none -> 141 us  [project(): pl.pallas_call(functools.partial(project_kernel, chips), out_shape=jax.Sh...]
    reduce_scatter x1 -> x0, waiting for transfers between devices: 131 us -> none  [per_device(): lax.psum_scatter(jnp.dot(attn, w_out, preferred_element_type=jnp.float32)...]
    dot_general x1 -> x0, matrix products: 24 us -> none  [per_device(): jnp.dot(attn, w_out, preferred_element_type=jnp.float32)]
    unnamed x17 -> x20, local copies, waits for them, and re-layouts: 4.54 us -> 8.26 us
    convert_element_type x0 -> x1, other arithmetic: none -> 3.71 us  [per_device(): (normed * norm_gain[None, :] * jax.nn.sigmoid(gate.astype(jnp.float32)))....]
  transfers between devices with their start and end apart: 2 -> 1, of which waited for: 1 -> 0; matrix products, arithmetic and copies ran while one was open for 13% -> 14% of each run, Pallas kernels for 0% -> 0%
where the time goes in v2:
time: 221 us; the launch traced here: 220 us
  Pallas kernels  141 us (64%)
  matrix products  33.8 us (15%)
  local copies, waits for them, and re-layouts  18.2 us (8%)
  between operations  13.5 us (6%)
  other arithmetic  13 us (6%)
    pallas_call x1, Pallas kernels, project(): pl.pallas_call(functools.partial(project_kernel, chips), out_shape=jax.Sh...  141 us
    dot_general x1, matrix products, per_device(): jnp.einsum('nhts,nshe->nthe', scores, va.astype(jnp.float32), precision=h...  18.3 us
    unnamed x20, local copies, waits for them, and re-layouts  8.26 us
    dot_general x1, matrix products, per_device(): jnp.einsum('nthd,nshd->nhts', qa, ka, preferred_element_type=jnp.float32)  8.18 us
    unnamed x2, other arithmetic  5.66 us
    add x1, local copies, waits for them, and re-layouts, per_device(): heads_out = (inter + intra).reshape(rows, heads, HD)  5.4 us
  transfers between devices with their start and end apart: 1, of which 0 were waited for; matrix products, arithmetic and copies ran while one was open for 14% of the time, Pallas kernels for 0%

profile of v2, /device:TPU:6, one launch (start us, length us, event | category | flops | bytes accessed | tf_op | source)
XLA Modules:
  0.0 219.5 jit_solution(15422719431552017978)
XLA Ops:
  6.5 0.0 all-gather.3.cloned.1.call-start
  6.5 2.8 %fusion.16 = bf16[128,8,8,128]{3,1,2,0:T(8,128)(2,1)S(1)} fusion(bf16[1024,1024]{1,0:T(8,128)(2,1)} %param.8), kind=kLoop, calls=%fused_computation.23 | loop fusion | flops 6291456 | bytes 4194304
  9.4 2.0 copy.37
  11.3 0.0 copy-done.5
  11.3 1.9 copy.38
  13.3 3.2 %copy.33 = bf16[2,512,8,128]{1,3,2,0:T(8,128)(2,1)S(1)} copy(bf16[2,512,8,128]{3,2,1,0:T(8,128)(2,1)} %bitcast.42) | data formatting | bytes 4194304 | tf_op jit(solution)/shard_map/reshape | solution.py:215
  16.4 3.2 %fusion.26 = (bf16[8,128,128]{2,1,0:T(8,128)(2,1)}, f32[2,8,128,128]{3,2,1,0:T(8,128)S(1)}) fusion(bf16[2,512,8,128]{1,3,2,0:T(8,128)(2,1)S(1)} %copy.33, bf16[2,512,8,128]{3,2,1,0:T(8,128)(2,1)} %bitcast.36), kind=kOutput, calls=%fused_computation.38 | convolution fusion | flops 268566528 | bytes 5505024 | tf_op jit(solution)/shard_map/nthd,nthe->nhde/dot_general | solution.py:216
  19.6 0.0 all-gather.3.cloned.1.call-update
  19.6 0.0 copy-start
  19.6 2.8 %fusion.15 = bf16[128,8,8,128]{3,1,2,0:T(8,128)(2,1)S(1)} fusion(bf16[1024,1024]{1,0:T(8,128)(2,1)} %param.7), kind=kLoop, calls=%fused_computation.22 | loop fusion | flops 6291456 | bytes 4194304
  22.5 0.6 copy.39
  23.1 0.0 copy-start.1
  23.1 0.0 copy-done
  23.1 8.2 %fusion.20 = f32[2,8,512,512]{3,2,1,0:T(8,128)} fusion(bf16[2,512,8,128]{3,2,1,0:T(8,128)(2,1)S(1)} %bitcast.37, bf16[2,512,8,128]{3,2,1,0:T(8,128)(2,1)S(1)} %bitcast.38), kind=kOutput, calls=%fused_computation.28 | convolution fusion | flops 1073741824 | bytes 20971520 | tf_op jit(solution)/shard_map/nthd,nshd->nhts/dot_general | solution.py:228
  31.3 0.0 copy-done.1
  31.3 0.1 iota_compare_fusion
  31.4 18.3 %fusion = f32[2,8,512,128]{2,3,1,0:T(8,128)} fusion(bf16[2,512,8,128]{1,3,2,0:T(8,128)(2,1)S(1)} %copy.33, f32[2,8,512,512]{3,2,1,0:T(8,128)} %fusion.20, pred[512,512]{1,0:T(8,128)(4,1)S(1)} %iota_compare_fusion), kind=kOutput, calls=%fused_computation | convolution fusion | flops 6446645248 | bytes 23330816 | tf_op jit(solution)/shard_map/nhts,nshe->nthe/dot_general | solution.py:231
  49.7 1.7 fusion.17
  51.4 1.5 add.37
  53.0 0.3 fusion.24
  53.2 0.0 copy-done.2
  53.2 0.0 copy-done.4
  53.3 4.1 %multiply_reduce_fusion = (f32[2,512,8]{1,2,0:T(8,128)S(1)}, f32[2,512,8,128]{1,3,2,0:T(8,128)}) fusion(f32[2,8,512,128]{2,3,1,0:T(8,128)S(1)} %copy-done.4, f32[2,8,128,128]{3,2,1,0:T(8,128)S(1)} %fusion.24, bf16[2,512,8,128]{3,2,1,0:T(8,128)(2,1)S(1)} %bitcast.39), kind=kOutput, calls=%fused_computation.21 | convolution fusion | flops 1613750272 | bytes 11567104 | tf_op jit(solution)/shard_map/nthd,nhde->nthe/dot_general | solution.py:227
  57.4 0.2 copy.35
  57.6 0.0 copy-start.6
  57.6 5.4 %copy.34 = f32[2,512,8,128]{3,2,1,0:T(8,128)} copy(f32[2,512,8,128]{1,3,2,0:T(8,128)} %get-tuple-element.8) | data formatting | bytes 8388608 | tf_op jit(solution)/shard_map/add | solution.py:232
  63.0 1.1 mul.46
  64.2 0.0 copy-done.6
  64.2 1.0 copy-done.3
  65.2 3.7 %fusion.14 = bf16[1024,1024]{1,0:T(8,128)(2,1)} fusion(f32[128,8,8,128]{3,2,1,0:T(8,128)S(1)} %bitcast.41, f32[128,8,8,128]{3,2,1,0:T(8,128)S(1)} %bitcast.40, bf16[1024,1024]{1,0:T(8,128)(2,1)S(1)} %copy-done.6, f32[1024]{0:T(1024)S(1)} %copy-done.7), kind=kLoop, calls=%fused_computation.19 | loop fusion | flops 8388608 | bytes 12587008 | tf_op jit(solution)/shard_map/convert_element_type | solution.py:235
  68.9 141.0 %shard_map.73 = bf16[128,6144]{1,0:T(8,128)(2,1)} custom-call(bf16[4,2,128,1024]{3,2,1,0:T(8,128)(2,1)} %bitcast.44, bf16[1024,6144]{1,0:T(8,128)(2,1)} %w_hbm.1), custom_call_target="tpu_custom_call" | custom-call | flops 12884901888 | bytes 12582912 | tf_op jit(solution)/shard_map/pallas_call | solution.py:178
  210.0 2.7 %copy.57 = bf16[128,6144]{1,0:T(8,128)(2,1)} copy(bf16[128,6144]{1,0:T(8,128)(2,1)} %shard_map.73) | data formatting | bytes 3145728
  (9 shorter events, 0.0 us)
Async XLA Ops:
  6.5 4.8 %copy-start.5 = (bf16[1024,1024]{1,0:T(8,128)(2,1)S(1)}, bf16[1024,1024]{1,0:T(8,128)(2,1)}, u32[]{:S(2)}) copy-start(bf16[1024,1024]{1,0:T(8,128)(2,1)} %param.9) | copy-start | bytes 6291460
  6.5 43.2 %all-gather.3.cloned.1.call-start = ((), (), s32[]{:S(2)}) async-start(), calls=%async_computation | async-start | bytes 1310720 | tf_op jit(solution)/shard_map/all_gather | solution.py:219
  19.6 3.5 %copy-start = (bf16[128,8,8,128]{3,2,1,0:T(8,128)(2,1)S(1)}, bf16[128,8,8,128]{3,2,1,0:T(8,128)(2,1)}, u32[]{:S(2)}) copy-start(bf16[128,8,8,128]{3,2,1,0:T(8,128)(2,1)} %copy.37) | copy-start | bytes 6291460
  23.1 8.2 %copy-start.1 = (bf16[128,8,8,128]{3,2,1,0:T(8,128)(2,1)}, bf16[128,8,8,128]{3,2,1,0:T(8,128)(2,1)S(1)}, u32[]{:S(2)}) copy-start(bf16[128,8,8,128]{3,2,1,0:T(8,128)(2,1)S(1)} %copy.39) | copy-start | bytes 6291460
  49.7 3.5 %copy-start.2 = (bf16[128,8,8,128]{3,2,1,0:T(8,128)(2,1)S(1)}, bf16[128,8,8,128]{3,2,1,0:T(8,128)(2,1)}, u32[]{:S(2)}) copy-start(bf16[128,8,8,128]{3,2,1,0:T(8,128)(2,1)} %copy-done.1) | copy-start | bytes 6291460
  49.7 3.5 %copy-start.4 = (f32[2,8,512,128]{2,3,1,0:T(8,128)S(1)}, f32[2,8,512,128]{2,3,1,0:T(8,128)}, u32[]{:S(2)}) copy-start(f32[2,8,512,128]{2,3,1,0:T(8,128)} %fusion) | copy-start | bytes 12582916
  57.6 6.6 %copy-start.6 = (bf16[1024,1024]{1,0:T(8,128)(2,1)S(1)}, bf16[1024,1024]{1,0:T(8,128)(2,1)}, u32[]{:S(2)}) copy-start(bf16[1024,1024]{1,0:T(8,128)(2,1)} %param.10) | copy-start | bytes 6291460
  63.0 2.2 copy-start.3
  63.0 2.2 copy-start.7
Sparse Core Ops, SparseCore 0:
  19.7 26.8 all-gather.2

commit v3 on v2

--- a/solution.py
+++ b/solution.py
@@ -12,7 +12,7 @@
 
 
 def project_kernel(
-    chips, a_ref, w_hbm, o_ref, w_ref, pair_out, pair_in, own, from_low, from_high, acc,
+    chips, a_ref, w_hbm, o_ref, w_ref, pair_out, pair_in, own, from_low, from_high,
     w_sem, pair_out_sem, pair_in_sem, up_sem, low_sem, down_sem, high_sem,
 ):
     pieces, depth, width = w_ref.shape
@@ -20,7 +20,9 @@
     me = lax.axis_index("tp")
     z, core = me // 2, me % 2
     sibling = me + 1 - 2 * core
-    top = chips - 1
+    above = lax.rem(z + 1, chips) * 2 + core
+    below = lax.rem(z + chips - 1, chips) * 2 + core
+    half = chips // 2
 
     def weights(k):
         return pltpu.make_async_copy(
@@ -31,17 +33,9 @@
         weights(k).start()
 
     barrier = pltpu.get_barrier_semaphore()
-    pl.semaphore_signal(barrier, inc=1, device_id={"tp": sibling}, device_id_type=MESH)
-
-    @pl.when(z > 0)
-    def _():
-        pl.semaphore_signal(barrier, inc=1, device_id={"tp": me - 2}, device_id_type=MESH)
-
-    @pl.when(z < top)
-    def _():
-        pl.semaphore_signal(barrier, inc=1, device_id={"tp": me + 2}, device_id_type=MESH)
-
-    pl.semaphore_wait(barrier, 1 + jnp.minimum(z, 1) + jnp.minimum(top - z, 1))
+    for peer in (sibling, above, below):
+        pl.semaphore_signal(barrier, inc=1, device_id={"tp": peer}, device_id_type=MESH)
+    pl.semaphore_wait(barrier, 3)
 
     def pair_copy(k):
         return pltpu.make_async_remote_copy(
@@ -50,18 +44,24 @@
             device_id={"tp": sibling}, device_id_type=MESH,
         )
 
-    def up_copy(k, j):
+    def owner_above(t):
+        return lax.rem(z + t, chips)
+
+    def owner_below(t):
+        return lax.rem(z + chips - t, chips)
+
+    def up_copy(k, t):
         return pltpu.make_async_remote_copy(
-            src_ref=own.at[k, top - j], dst_ref=from_low.at[k, j],
-            send_sem=up_sem.at[k, j], recv_sem=low_sem.at[k, j],
-            device_id={"tp": me + 2}, device_id_type=MESH,
-        )
-
-    def down_copy(k, j):
+            src_ref=own.at[k, owner_above(t)], dst_ref=from_low.at[k, t - 1],
+            send_sem=up_sem.at[k, t - 1], recv_sem=low_sem.at[k, t - 1],
+            device_id={"tp": above}, device_id_type=MESH,
+        )
+
+    def down_copy(k, t):
         return pltpu.make_async_remote_copy(
-            src_ref=own.at[k, j], dst_ref=from_high.at[k, j],
-            send_sem=down_sem.at[k, j], recv_sem=high_sem.at[k, j],
-            device_id={"tp": me - 2}, device_id_type=MESH,
+            src_ref=own.at[k, owner_below(t)], dst_ref=from_high.at[k, t - 1],
+            send_sem=down_sem.at[k, t - 1], recv_sem=high_sem.at[k, t - 1],
+            device_id={"tp": below}, device_id_type=MESH,
         )
 
     def partial(k, side):
@@ -78,87 +78,74 @@
     def chip_sum(k, d):
         return own[k, d].astype(jnp.float32) + pair_in[k, d].astype(jnp.float32)
 
+    def forward(k, t, first, copy, owner, arrived):
+        def begin():
+            d = owner(t)
+            own[k, d] = chip_sum(k, d).astype(own.dtype)
+            copy(k, t).start()
+
+        def relay():
+            d = owner(t)
+            copy(k, t + 1).wait_recv()
+            total = chip_sum(k, d) + arrived[k, t].astype(jnp.float32)
+            own[k, d] = total.astype(own.dtype)
+            copy(k, t).start()
+
+        if t == half:
+            pl.when(first)(begin)
+        elif t == half - 1:
+            pl.when(first)(relay)
+            pl.when(jnp.logical_not(first))(begin)
+        else:
+            relay()
+
     def pass_on(k):
         pair_copy(k).wait_recv()
-        for j in range(top):
-            up, down = top - j, j
-
-            @pl.when(up > z)
-            def _():
-                @pl.when(z > 0)
-                def _():
-                    up_copy(k, j).wait_recv()
-                    total = chip_sum(k, up) + from_low[k, j].astype(jnp.float32)
-                    own[k, up] = total.astype(own.dtype)
-
-                @pl.when(z == 0)
-                def _():
-                    own[k, up] = chip_sum(k, up).astype(own.dtype)
-
-                @pl.when(k >= 1)
-                def _():
-                    up_copy(k - 1, j).wait_send()
-
-                up_copy(k, j).start()
-
-            @pl.when(down < z)
-            def _():
-                @pl.when(z < top)
-                def _():
-                    down_copy(k, j).wait_recv()
-                    total = chip_sum(k, down) + from_high[k, j].astype(jnp.float32)
-                    own[k, down] = total.astype(own.dtype)
-
-                @pl.when(z == top)
-                def _():
-                    own[k, down] = chip_sum(k, down).astype(own.dtype)
-
-                @pl.when(k >= 1)
-                def _():
-                    down_copy(k - 1, j).wait_send()
-
-                down_copy(k, j).start()
+        even = k % 2 == 0
+        for t in range(half, 0, -1):
+            forward(k, t, even, up_copy, owner_above, from_low)
+            forward(k, t, jnp.logical_not(even), down_copy, owner_below, from_high)
 
     def finish(k):
-        acc[...] = chip_sum(k, z)
-
-        @pl.when(z < top)
-        def _():
-            down_copy(k, z).wait_recv()
-            acc[...] = acc[...] + from_high[k, z].astype(jnp.float32)
-
-        @pl.when(z > 0)
-        def _():
-            up_copy(k, top - z).wait_recv()
-            acc[...] = acc[...] + from_low[k, top - z].astype(jnp.float32)
-
-        o_ref[:, pl.ds(pl.multiple_of(k * width, width), width)] = acc[...].astype(o_ref.dtype)
+        up_copy(k, 1).wait_recv()
+        down_copy(k, 1).wait_recv()
+        total = chip_sum(k, z) + from_low[k, 0].astype(jnp.float32)
+        total = total + from_high[k, 0].astype(jnp.float32)
+        o_ref[:, pl.ds(pl.multiple_of(k * width, width), width)] = total.astype(o_ref.dtype)
+
+    def sent(k):
+        for t in range(half - 1, 0, -1):
+            up_copy(k, t).wait_send()
+            down_copy(k, t).wait_send()
+
+        @pl.when(k % 2 == 0)
+        def _():
+            up_copy(k, half).wait_send()
+
+        @pl.when(k % 2 == 1)
+        def _():
+            down_copy(k, half).wait_send()
 
     def step(k, carry):
         @pl.when(k < pieces)
         def _():
             compute(k)
 
+        @pl.when((k >= 3) & (k <= pieces + 2))
+        def _():
+            sent(k - 3)
+
         @pl.when((k >= 1) & (k <= pieces))
         def _():
             pass_on(k - 1)
 
-        @pl.when(k >= 2)
+        @pl.when((k >= 2) & (k <= pieces + 1))
         def _():
             finish(k - 2)
 
         return carry
 
-    lax.fori_loop(0, pieces + 2, step, 0)
-
-    for j in range(top):
-        @pl.when(top - j > z)
-        def _():
-            up_copy(pieces - 1, j).wait_send()
-
-        @pl.when(j < z)
-        def _():
-            down_copy(pieces - 1, j).wait_send()
+    lax.fori_loop(0, pieces + 3, step, 0)
 
     def drain(k, carry):
         pair_copy(k).wait_send()
@@ -182,11 +169,10 @@
         out_specs=pl.BlockSpec(memory_space=pltpu.VMEM),
         scratch_shapes=[
             pltpu.VMEM((pieces, depth, width), jnp.bfloat16),
-            chunk(chips), chunk(chips), chunk(chips), chunk(chips - 1), chunk(chips - 1),
-            pltpu.VMEM((rows, width), jnp.float32),
+            chunk(chips), chunk(chips), chunk(chips), chunk(chips // 2), chunk(chips // 2),
             dma(pieces), dma(pieces), dma(pieces),
-            dma(pieces, chips - 1), dma(pieces, chips - 1),
-            dma(pieces, chips - 1), dma(pieces, chips - 1),
+            dma(pieces, chips // 2), dma(pieces, chips // 2),
+            dma(pieces, chips // 2), dma(pieces, chips // 2),
         ],
         compiler_params=pltpu.CompilerParams(
             collective_id=0, has_side_effects=True, vmem_limit_bytes=60 * 2**20

time: 221 us -> 203 us (0.919)
  Pallas kernels: 141 us -> 123 us
    pallas_call x1, Pallas kernels: 141 us -> 123 us  [project(): pl.pallas_call(functools.partial(project_kernel, chips), out_shape=jax.Sh...]
  transfers between devices with their start and end apart: 1 -> 1, of which waited for: 0 -> 0; matrix products, arithmetic and copies ran while one was open for 14% -> 15% of each run, Pallas kernels for 0% -> 0%
where the time goes in v3:
time: 203 us; the launch traced here: 202 us
  Pallas kernels  123 us (61%)
  matrix products  33.8 us (17%)
  local copies, waits for them, and re-layouts  18.2 us (9%)
  between operations  13.5 us (7%)
  other arithmetic  13 us (6%)
    pallas_call x1, Pallas kernels, project(): pl.pallas_call(functools.partial(project_kernel, chips), out_shape=jax.Sh...  123 us
    dot_general x1, matrix products, per_device(): jnp.einsum('nhts,nshe->nthe', scores, va.astype(jnp.float32), precision=h...  18.3 us
    unnamed x20, local copies, waits for them, and re-layouts  8.26 us
    dot_general x1, matrix products, per_device(): jnp.einsum('nthd,nshd->nhts', qa, ka, preferred_element_type=jnp.float32)  8.18 us
    unnamed x2, other arithmetic  5.66 us
    add x1, local copies, waits for them, and re-layouts, per_device(): heads_out = (inter + intra).reshape(rows, heads, HD)  5.4 us
    dot_general x1, matrix products, per_device(): inter = jnp.einsum('nthd,nhde->nthe', q_float, states, precision=highest)  4.14 us
  transfers between devices with their start and end apart: 1, of which 0 were waited for; matrix products, arithmetic and copies ran while one was open for 15% of the time, Pallas kernels for 0%

profile of v3, /device:TPU:6, one launch (start us, length us, event | category | flops | bytes accessed | tf_op | source)
XLA Modules:
  0.0 201.6 jit_solution(5853913248424601704)
XLA Ops:
  6.5 0.0 all-gather.3.cloned.1.call-start
  6.5 2.8 %fusion.16 = bf16[128,8,8,128]{3,1,2,0:T(8,128)(2,1)S(1)} fusion(bf16[1024,1024]{1,0:T(8,128)(2,1)} %param.8), kind=kLoop, calls=%fused_computation.23 | loop fusion | flops 6291456 | bytes 4194304
  9.4 2.0 copy.37
  11.3 0.0 copy-done.5
  11.3 1.9 copy.38
  13.3 3.2 %copy.33 = bf16[2,512,8,128]{1,3,2,0:T(8,128)(2,1)S(1)} copy(bf16[2,512,8,128]{3,2,1,0:T(8,128)(2,1)} %bitcast.42) | data formatting | bytes 4194304 | tf_op jit(solution)/shard_map/reshape | solution.py:201
  16.4 3.2 %fusion.26 = (bf16[8,128,128]{2,1,0:T(8,128)(2,1)}, f32[2,8,128,128]{3,2,1,0:T(8,128)S(1)}) fusion(bf16[2,512,8,128]{1,3,2,0:T(8,128)(2,1)S(1)} %copy.33, bf16[2,512,8,128]{3,2,1,0:T(8,128)(2,1)} %bitcast.36), kind=kOutput, calls=%fused_computation.38 | convolution fusion | flops 268566528 | bytes 5505024 | tf_op jit(solution)/shard_map/nthd,nthe->nhde/dot_general | solution.py:202
  19.6 0.0 all-gather.3.cloned.1.call-update
  19.6 0.0 copy-start
  19.6 2.8 %fusion.15 = bf16[128,8,8,128]{3,1,2,0:T(8,128)(2,1)S(1)} fusion(bf16[1024,1024]{1,0:T(8,128)(2,1)} %param.7), kind=kLoop, calls=%fused_computation.22 | loop fusion | flops 6291456 | bytes 4194304
  22.5 0.6 copy.39
  23.1 0.0 copy-start.1
  23.1 0.0 copy-done
  23.1 8.2 %fusion.20 = f32[2,8,512,512]{3,2,1,0:T(8,128)} fusion(bf16[2,512,8,128]{3,2,1,0:T(8,128)(2,1)S(1)} %bitcast.37, bf16[2,512,8,128]{3,2,1,0:T(8,128)(2,1)S(1)} %bitcast.38), kind=kOutput, calls=%fused_computation.28 | convolution fusion | flops 1073741824 | bytes 20971520 | tf_op jit(solution)/shard_map/nthd,nshd->nhts/dot_general | solution.py:214
  31.3 0.0 copy-done.1
  31.3 0.1 iota_compare_fusion
  31.4 18.3 %fusion = f32[2,8,512,128]{2,3,1,0:T(8,128)} fusion(bf16[2,512,8,128]{1,3,2,0:T(8,128)(2,1)S(1)} %copy.33, f32[2,8,512,512]{3,2,1,0:T(8,128)} %fusion.20, pred[512,512]{1,0:T(8,128)(4,1)S(1)} %iota_compare_fusion), kind=kOutput, calls=%fused_computation | convolution fusion | flops 6446645248 | bytes 23330816 | tf_op jit(solution)/shard_map/nhts,nshe->nthe/dot_general | solution.py:217
  49.7 1.7 fusion.17
  51.4 1.5 add.37
  53.0 0.3 fusion.24
  53.2 0.0 copy-done.2
  53.2 0.0 copy-done.4
  53.3 4.1 %multiply_reduce_fusion = (f32[2,512,8]{1,2,0:T(8,128)S(1)}, f32[2,512,8,128]{1,3,2,0:T(8,128)}) fusion(f32[2,8,512,128]{2,3,1,0:T(8,128)S(1)} %copy-done.4, f32[2,8,128,128]{3,2,1,0:T(8,128)S(1)} %fusion.24, bf16[2,512,8,128]{3,2,1,0:T(8,128)(2,1)S(1)} %bitcast.39), kind=kOutput, calls=%fused_computation.21 | convolution fusion | flops 1613750272 | bytes 11567104 | tf_op jit(solution)/shard_map/nthd,nhde->nthe/dot_general | solution.py:213
  57.4 0.2 copy.35
  57.6 0.0 copy-start.6
  57.6 5.4 %copy.34 = f32[2,512,8,128]{3,2,1,0:T(8,128)} copy(f32[2,512,8,128]{1,3,2,0:T(8,128)} %get-tuple-element.8) | data formatting | bytes 8388608 | tf_op jit(solution)/shard_map/add | solution.py:218
  63.0 1.1 mul.46
  64.2 1.0 copy-done.3
  65.2 0.0 copy-done.7
  65.2 3.7 %fusion.14 = bf16[1024,1024]{1,0:T(8,128)(2,1)} fusion(f32[128,8,8,128]{3,2,1,0:T(8,128)S(1)} %bitcast.41, f32[128,8,8,128]{3,2,1,0:T(8,128)S(1)} %bitcast.40, bf16[1024,1024]{1,0:T(8,128)(2,1)S(1)} %copy-done.6, f32[1024]{0:T(1024)S(1)} %copy-done.7), kind=kLoop, calls=%fused_computation.19 | loop fusion | flops 8388608 | bytes 12587008 | tf_op jit(solution)/shard_map/convert_element_type | solution.py:221
  68.9 123.1 %shard_map.73 = bf16[128,6144]{1,0:T(8,128)(2,1)} custom-call(bf16[4,2,128,1024]{3,2,1,0:T(8,128)(2,1)} %bitcast.44, bf16[1024,6144]{1,0:T(8,128)(2,1)} %w_hbm.1), custom_call_target="tpu_custom_call" | custom-call | flops 12884901888 | bytes 12582912 | tf_op jit(solution)/shard_map/pallas_call | solution.py:165
  192.0 2.7 %copy.57 = bf16[128,6144]{1,0:T(8,128)(2,1)} copy(bf16[128,6144]{1,0:T(8,128)(2,1)} %shard_map.73) | data formatting | bytes 3145728
  (9 shorter events, 0.0 us)
Async XLA Ops:
  6.5 4.8 %copy-start.5 = (bf16[1024,1024]{1,0:T(8,128)(2,1)S(1)}, bf16[1024,1024]{1,0:T(8,128)(2,1)}, u32[]{:S(2)}) copy-start(bf16[1024,1024]{1,0:T(8,128)(2,1)} %param.9) | copy-start | bytes 6291460
  6.5 43.2 %all-gather.3.cloned.1.call-start = ((), (), s32[]{:S(2)}) async-start(), calls=%async_computation | async-start | bytes 1310720 | tf_op jit(solution)/shard_map/all_gather | solution.py:205
  19.6 3.5 %copy-start = (bf16[128,8,8,128]{3,2,1,0:T(8,128)(2,1)S(1)}, bf16[128,8,8,128]{3,2,1,0:T(8,128)(2,1)}, u32[]{:S(2)}) copy-start(bf16[128,8,8,128]{3,2,1,0:T(8,128)(2,1)} %copy.37) | copy-start | bytes 6291460
  23.1 8.2 %copy-start.1 = (bf16[128,8,8,128]{3,2,1,0:T(8,128)(2,1)}, bf16[128,8,8,128]{3,2,1,0:T(8,128)(2,1)S(1)}, u32[]{:S(2)}) copy-start(bf16[128,8,8,128]{3,2,1,0:T(8,128)(2,1)S(1)} %copy.39) | copy-start | bytes 6291460
  49.7 3.5 %copy-start.2 = (bf16[128,8,8,128]{3,2,1,0:T(8,128)(2,1)S(1)}, bf16[128,8,8,128]{3,2,1,0:T(8,128)(2,1)}, u32[]{:S(2)}) copy-start(bf16[128,8,8,128]{3,2,1,0:T(8,128)(2,1)} %copy-done.1) | copy-start | bytes 6291460
  49.7 3.5 %copy-start.4 = (f32[2,8,512,128]{2,3,1,0:T(8,128)S(1)}, f32[2,8,512,128]{2,3,1,0:T(8,128)}, u32[]{:S(2)}) copy-start(f32[2,8,512,128]{2,3,1,0:T(8,128)} %fusion) | copy-start | bytes 12582916
  57.6 6.6 %copy-start.6 = (bf16[1024,1024]{1,0:T(8,128)(2,1)S(1)}, bf16[1024,1024]{1,0:T(8,128)(2,1)}, u32[]{:S(2)}) copy-start(bf16[1024,1024]{1,0:T(8,128)(2,1)} %param.10) | copy-start | bytes 6291460
  63.0 2.2 %copy-start.3 = (f32[2,512,8,128]{3,2,1,0:T(8,128)S(1)}, f32[2,512,8,128]{3,2,1,0:T(8,128)}, u32[]{:S(2)}) copy-start(f32[2,512,8,128]{3,2,1,0:T(8,128)} %copy.34) | copy-start | bytes 12582916
  63.0 2.2 %copy-start.7 = (f32[1024]{0:T(1024)S(1)}, f32[1024]{0:T(1024)}, u32[]{:S(2)}) copy-start(f32[1024]{0:T(1024)} %param.12) | copy-start | bytes 12292
Sparse Core Ops, SparseCore 0:
  19.7 26.8 all-gather.2

commit v4 on v3

--- a/solution.py
+++ b/solution.py
@@ -9,6 +9,145 @@
 
 HD = 128
 MESH = pl.DeviceIdType.MESH
+
+
+def sigmoid(u):
+    return 0.5 + 0.5 * jnp.tanh(0.5 * u)
+
+
+def attend_kernel(
+    n_seq, block, q_ref, k_ref, v_ref, g_ref, kv_ref, gain_ref, o_ref,
+    qa_ref, ka_ref, local, prefix, state, own_sum, arrived, send_sem, recv_sem,
+):
+    me = lax.axis_index("seq")
+    heads = kv_ref.shape[0]
+    count = q_ref.shape[0] // block
+    blocks = [slice(n * block, (n + 1) * block) for n in range(count)]
+    f32 = jnp.float32
+
+    barrier = pltpu.get_barrier_semaphore()
+    for p in range(n_seq):
+        @pl.when(p != me)
+        def _():
+            pl.semaphore_signal(barrier, inc=1, device_id={"seq": p}, device_id_type=MESH)
+
+    def lanes(h):
+        return pl.ds(pl.multiple_of(h * HD, HD), HD)
+
+    def sums(h, carry):
+        total = jnp.zeros((HD, HD), f32)
+        for n, rows in enumerate(blocks):
+            u = k_ref[rows, lanes(h)].astype(f32)
+            ka = (u * sigmoid(u)).astype(jnp.bfloat16)
+            ka_ref[rows, lanes(h)] = ka
+            prefix[h, n] = total.astype(jnp.bfloat16)
+            total += lax.dot_general(
+                ka, v_ref[rows, lanes(h)], (((0,), (0,)), ((), ())), preferred_element_type=f32
+            )
+        own_sum[h] = total.astype(jnp.bfloat16)
+        return carry
+
+    lax.fori_loop(0, heads, sums, 0)
+    pl.semaphore_wait(barrier, n_seq - 1)
+
+    def copy_to(p):
+        return pltpu.make_async_remote_copy(
+            src_ref=own_sum, dst_ref=arrived.at[me],
+            send_sem=send_sem.at[p], recv_sem=recv_sem.at[me],
+            device_id={"seq": p}, device_id_type=MESH,
+        )
+
+    def copy_from(p):
+        return pltpu.make_async_remote_copy(
+            src_ref=own_sum, dst_ref=arrived.at[p],
+            send_sem=send_sem.at[p], recv_sem=recv_sem.at[p],
+            device_id={"seq": p}, device_id_type=MESH,
+        )
+
+    for p in range(n_seq - 1, -1, -1):
+        @pl.when(p > me)
+        def _():
+            copy_to(p).start()
+
+    above = lax.broadcasted_iota(jnp.int32, (block, block), 0) >= lax.broadcasted_iota(
+        jnp.int32, (block, block), 1
+    )
+
+    def within(h, carry):
+        for n, rows in enumerate(blocks):
+            u = q_ref[rows, lanes(h)].astype(f32)
+            qa = (u * sigmoid(u)).astype(jnp.bfloat16)
+            qa_ref[rows, lanes(h)] = qa
+            scores = lax.dot_general(
+                qa, ka_ref[rows, lanes(h)], (((1,), (1,)), ((), ())), preferred_element_type=f32
+            )
+            scores = jnp.where(above, scores, 0.0).astype(jnp.bfloat16)
+            out = jnp.dot(scores, v_ref[rows, lanes(h)], preferred_element_type=f32)
+            if n > 0:
+                out += jnp.dot(qa, prefix[h, n], preferred_element_type=f32)
+            local[rows, lanes(h)] = out
+        return carry
+
+    lax.fori_loop(0, heads, within, 0)
+
+    state[...] = kv_ref[...]
+    for p in range(n_seq):
+        @pl.when(p < me)
+        def _():
+            copy_from(p).wait_recv()
+            state[...] += arrived[p].astype(f32)
+
+    def outputs(h, carry):
+        high = state[h].astype(jnp.bfloat16)
+        low = (state[h] - high.astype(f32)).astype(jnp.bfloat16)
+        gain = gain_ref[:, lanes(h)]
+        for rows in blocks:
+            qa = qa_ref[rows, lanes(h)]
+            out = local[rows, lanes(h)] + jnp.dot(qa, high, preferred_element_type=f32)
+            out += jnp.dot(qa, low, preferred_element_type=f32)
+            scale = lax.rsqrt(jnp.mean(out * out, axis=-1, keepdims=True) + 1e-05)
+            gate = sigmoid(g_ref[rows, lanes(h)].astype(f32))
+            o_ref[rows, lanes(h)] = (out * scale * gain * gate).astype(o_ref.dtype)
+        return carry
+
+    lax.fori_loop(0, heads, outputs, 0)
+
+    for p in range(n_seq):
+        @pl.when(p > me)
+        def _():
+            copy_to(p).wait_send()
+
+
+def attend(query, key_in, value, gate, kv_start, norm_gain, n_seq):
+    rows, columns = query.shape
+    heads = columns // HD
+    block = min(256, rows)
+    vmem = pl.BlockSpec(memory_space=pltpu.VMEM)
+    bf16, f32 = jnp.bfloat16, jnp.float32
+    return pl.pallas_call(
+        functools.partial(attend_kernel, n_seq, block),
+        out_shape=jax.ShapeDtypeStruct((rows, columns), bf16),
+        in_specs=[vmem] * 6,
+        out_specs=vmem,
+        scratch_shapes=[
+            pltpu.VMEM((rows, columns), bf16),
+            pltpu.VMEM((rows, columns), bf16),
+            pltpu.VMEM((rows, columns), f32),
+            pltpu.VMEM((heads, rows // block, HD, HD), bf16),
+            pltpu.VMEM((heads, HD, HD), f32),
+            pltpu.VMEM((heads, HD, HD), bf16),
+            pltpu.VMEM((n_seq, heads, HD, HD), bf16),
+            pltpu.SemaphoreType.DMA((n_seq,)),
+            pltpu.SemaphoreType.DMA((n_seq,)),
+        ],
+        compiler_params=pltpu.CompilerParams(
+            collective_id=1, has_side_effects=True, vmem_limit_bytes=60 * 2**20
+        ),
+        cost_estimate=pl.CostEstimate(
+            flops=8 * rows * block * columns, bytes_accessed=10 * rows * columns,
+            transcendentals=3 * rows * columns,
+        ),
+    )(query, key_in, value, gate, kv_start, norm_gain.reshape(1, columns))
 
 
 def project_kernel(
@@ -78,33 +217,43 @@
     def chip_sum(k, d):
         return own[k, d].astype(jnp.float32) + pair_in[k, d].astype(jnp.float32)
 
-    def forward(k, t, first, copy, owner, arrived):
-        def begin():
-            d = owner(t)
-            own[k, d] = chip_sum(k, d).astype(own.dtype)
-            copy(k, t).start()
-
-        def relay():
-            d = owner(t)
-            copy(k, t + 1).wait_recv()
-            total = chip_sum(k, d) + arrived[k, t].astype(jnp.float32)
-            own[k, d] = total.astype(own.dtype)
-            copy(k, t).start()
-
-        if t == half:
-            pl.when(first)(begin)
-        elif t == half - 1:
-            pl.when(first)(relay)
-            pl.when(jnp.logical_not(first))(begin)
+    def begin(k, t, copy, owner):
+        d = owner(t)
+        own[k, d] = chip_sum(k, d).astype(own.dtype)
+        copy(k, t).start()
+
+    def relay(k, t, copy, owner, arrived):
+        d = owner(t)
+        copy(k, t + 1).wait_recv()
+        total = chip_sum(k, d) + arrived[k, t].astype(jnp.float32)
+        own[k, d] = total.astype(own.dtype)
+        copy(k, t).start()
+
+    def send_first(k):
+        pair_copy(k).wait_recv()
+
+        @pl.when(k % 2 == 0)
+        def _():
+            begin(k, half, up_copy, owner_above)
+            begin(k, half - 1, down_copy, owner_below)
+
+        @pl.when(k % 2 == 1)
+        def _():
+            begin(k, half, down_copy, owner_below)
+            begin(k, half - 1, up_copy, owner_above)
+
+    def send_on(k, t):
+        if t < half - 1:
+            relay(k, t, up_copy, owner_above, from_low)
+            relay(k, t, down_copy, owner_below, from_high)
         else:
-            relay()
-
-    def pass_on(k):
-        pair_copy(k).wait_recv()
-        even = k % 2 == 0
-        for t in range(half, 0, -1):
-            forward(k, t, even, up_copy, owner_above, from_low)
-            forward(k, t, jnp.logical_not(even), down_copy, owner_below, from_high)
+            @pl.when(k % 2 == 0)
+            def _():
+                relay(k, t, up_copy, owner_above, from_low)
+
+            @pl.when(k % 2 == 1)
+            def _():
+                relay(k, t, down_copy, owner_below, from_high)
 
     def finish(k):
         up_copy(k, 1).wait_recv()
@@ -127,25 +276,18 @@
             down_copy(k, half).wait_send()
 
     def step(k, carry):
-        @pl.when(k < pieces)
-        def _():
-            compute(k)
-
-        @pl.when((k >= 3) & (k <= pieces + 2))
-        def _():
-            sent(k - 3)
-
-        @pl.when((k >= 1) & (k <= pieces))
-        def _():
-            pass_on(k - 1)
-
-        @pl.when((k >= 2) & (k <= pieces + 1))
-        def _():
-            finish(k - 2)
-
-        return carry
-
-    lax.fori_loop(0, pieces + 3, step, 0)
+        def at(lag, work):
+            pl.when((k >= lag) & (k < pieces + lag))(lambda: work(k - lag))
+
+        at(0, compute)
+        at(half + 2, sent)
+        at(1, send_first)
+        for t in range(half - 1, 0, -1):
+            at(1 + half - t, functools.partial(send_on, t=t))
+        at(half + 1, finish)
+        return carry
+
+    lax.fori_loop(0, pieces + half + 2, step, 0)
 
     def drain(k, carry):
         pair_copy(k).wait_send()
@@ -184,43 +326,8 @@
     )(attn.reshape(chips, 2, rows, depth), w_out)
 
 
-def per_device(n_tp, query, key_in, value, gate, kv_start, norm_gain, w_out):
-    rows = query.shape[0]
-    heads = query.shape[1] // HD
-    block = min(512, rows)
-    count = rows // block
-    highest = lax.Precision.HIGHEST
-    qa = (
-        jax.nn.silu(query.astype(jnp.float32)).astype(jnp.bfloat16).reshape(count, block, heads, HD)
-    )
-    ka = (
-        jax.nn.silu(key_in.astype(jnp.float32))
-        .astype(jnp.bfloat16)
-        .reshape(count, block, heads, HD)
-    )
-    va = value.reshape(count, block, heads, HD)
-    block_states = jnp.einsum("nthd,nthe->nhde", ka, va, preferred_element_type=jnp.float32)
-    own_total = jnp.sum(block_states, axis=0)
-    local_before = jnp.cumsum(block_states, axis=0) - block_states
-    gathered = lax.all_gather(
-        own_total[None].astype(jnp.bfloat16), "seq", axis=0, tiled=True
-    ).astype(jnp.float32)
-    position = lax.axis_index("seq")
-    below = (jnp.arange(gathered.shape[0]) < position).astype(jnp.float32)
-    prior = jnp.sum(gathered * below[:, None, None, None], axis=0)
-    states = local_before + (kv_start + prior)[None]
-    q_float = qa.astype(jnp.float32)
-    inter = jnp.einsum("nthd,nhde->nthe", q_float, states, precision=highest)
-    scores = jnp.einsum("nthd,nshd->nhts", qa, ka, preferred_element_type=jnp.float32)
-    causal = jnp.arange(block)[:, None] >= jnp.arange(block)[None, :]
-    scores = jnp.where(causal[None, None], scores, jnp.float32(0.0))
-    intra = jnp.einsum("nhts,nshe->nthe", scores, va.astype(jnp.float32), precision=highest)
-    heads_out = (inter + intra).reshape(rows, heads, HD)
-    scale = lax.rsqrt(jnp.mean(heads_out * heads_out, axis=-1, keepdims=True) + 1e-05)
-    normed = (heads_out * scale).reshape(rows, heads * HD)
-    attn = (normed * norm_gain[None, :] * jax.nn.sigmoid(gate.astype(jnp.float32))).astype(
-        jnp.bfloat16
-    )
+def per_device(n_seq, n_tp, query, key_in, value, gate, kv_start, norm_gain, w_out):
+    attn = attend(query, key_in, value, gate, kv_start, norm_gain, n_seq)
     return project(attn, w_out, n_tp)
 
 
@@ -236,5 +343,5 @@
     )
     out_specs = P(("seq", "tp"), None)
     return jax.shard_map(
-        functools.partial(per_device, mesh.shape["tp"]), mesh=mesh, in_specs=in_specs, out_specs=out_specs, check_vma=False
+        functools.partial(per_device, mesh.shape["seq"], mesh.shape["tp"]), mesh=mesh, in_specs=in_specs, out_specs=out_specs, check_vma=False
     )

time: 203 us -> 141 us (0.69)
  matrix products: 33.8 us -> 0 us
  local copies, waits for them, and re-layouts: 18.2 us -> 2.69 us
  Pallas kernels: 123 us -> 138 us
  between operations: 13.5 us -> 0.02 us
  other arithmetic: 13 us -> 0 us
    dot_general x4 -> x0, matrix products: 33.8 us -> none  [the longest x1 18.3 us: per_device(): jnp.einsum('nhts,nshe->nthe', scores, va.astype(jnp.float32), precision=h...]
    pallas_call x0 -> x1, Pallas kernels: none -> 23.3 us  [attend(): pl.pallas_call(functools.partial(attend_kernel, n_seq, block), out_shape=...]
    pallas_call x1, Pallas kernels: 123 us -> 115 us  [project(): pl.pallas_call(functools.partial(project_kernel, chips), out_shape=jax.Sh...]
    unnamed x2 -> x0, other arithmetic: 5.66 us -> none
    unnamed x20 -> x1, local copies, waits for them, and re-layouts: 8.26 us -> 2.69 us
    add x1 -> x0, local copies, waits for them, and re-layouts: 5.4 us -> none  [per_device(): heads_out = (inter + intra).reshape(rows, heads, HD)]
    convert_element_type x2 -> x0, other arithmetic: 3.72 us -> none  [the longest x1 3.71 us: per_device(): (normed * norm_gain[None, :] * jax.nn.sigmoid(gate.astype(jnp.float32)))....]
    reshape x1 -> x0, local copies, waits for them, and re-layouts: 3.17 us -> none  [per_device(): va = value.reshape(count, block, heads, HD)]
  transfers between devices with their start and end apart: 1 -> 0, of which waited for: 0 -> 0; matrix products, arithmetic and copies ran while one was open for 15% -> 0% of each run, Pallas kernels for 0% -> 0%
where the time goes in v4:
time: 141 us
  Pallas kernels  138 us (98%)
  local copies, waits for them, and re-layouts  2.69 us (2%)
    pallas_call x1, Pallas kernels, project(): pl.pallas_call(functools.partial(project_kernel, chips), out_shape=jax.Sh...  115 us
    pallas_call x1, Pallas kernels, attend(): pl.pallas_call(functools.partial(attend_kernel, n_seq, block), out_shape=...  23.3 us

profile of v4, /device:TPU:6, one launch (start us, length us, event | category | flops | bytes accessed | tf_op | source)
XLA Modules:
  0.0 140.7 jit_solution(3696082873445417941)
XLA Ops:
  0.0 23.3 %shard_map.73 = bf16[1024,1024]{1,0:T(8,128)(2,1)} custom-call(bf16[1024,1024]{1,0:T(8,128)(2,1)} %q_ref.1, bf16[1024,1024]{1,0:T(8,128)(2,1)} %k_ref.1, bf16[1024,1024]{1,0:T(8,128)(2,1)} %v_ref.1, bf16[1024,1024]{1,0:T(8,128)(2,1)} %g_ref.1, f32[8,128,128]{2,1,0:T(8,128)} %kv_ref.1, f32[1,1024]{1,0:T(1,128)} %bitcast.3), custom_call_target="tpu_custom_call" | custom-call | flops 2147483648 | bytes 10485760 | tf_op jit(solution)/shard_map/pallas_call | solution.py:127
  23.3 114.6 %shard_map.74 = bf16[128,6144]{1,0:T(8,128)(2,1)} custom-call(bf16[4,2,128,1024]{3,2,1,0:T(8,128)(2,1)} %bitcast.2, bf16[1024,6144]{1,0:T(8,128)(2,1)} %w_hbm.1), custom_call_target="tpu_custom_call" | custom-call | flops 12884901888 | bytes 12582912 | tf_op jit(solution)/shard_map/pallas_call | solution.py:307
  138.0 2.7 %copy.9 = bf16[128,6144]{1,0:T(8,128)(2,1)} copy(bf16[128,6144]{1,0:T(8,128)(2,1)} %shard_map.74) | data formatting | bytes 3145728

commit v5 on v3

v5 whole, which is shorter than its diff:
```python
import functools

import jax
import jax.numpy as jnp
from jax import lax
from jax.experimental import pallas as pl
from jax.experimental.pallas import tpu as pltpu
from jax.sharding import PartitionSpec as P

HD = 128
MESH = pl.DeviceIdType.MESH


def sigmoid(u):
    return 0.5 + 0.5 * jnp.tanh(0.5 * u)


def layer_kernel(
    n_seq, chips, block, q_hbm, k_hbm, v_hbm, g_hbm, kv_ref, gain_ref, w_hbm, o_ref,
    q_ref, k_ref, v_ref, a_ref, local, prefix, state, own_sum, arrived,
    w_ref, pair_out, pair_in, own, from_low, from_high,
    qg_sem, kv_sem, send_sem, recv_sem,
    w_sem, pair_out_sem, pair_in_sem, up_sem, low_sem, down_sem, high_sem,
):
    f32, bf16 = jnp.float32, jnp.bfloat16
    heads = kv_ref.shape[0]
    part = heads // 2
    blocks = [slice(n * block, (n + 1) * block) for n in range(q_ref.shape[0] // block)]
    pieces, depth, width = w_ref.shape
    rows = o_ref.shape[0]
    at_seq = lax.axis_index("seq")
    me = lax.axis_index("tp")
    z, core = me // 2, me % 2
    sibling = me + 1 - 2 * core
    above = lax.rem(z + 1, chips) * 2 + core
    below = lax.rem(z + chips - 1, chips) * 2 + core
    half = chips // 2

    def lanes(h):
        return pl.ds(pl.multiple_of(h * HD, HD), HD)

    def load_head(i, h):
        hbm, ref = ((k_hbm, k_ref), (v_hbm, v_ref))[i]
        return pltpu.make_async_copy(hbm.at[:, lanes(h)], ref.at[:, lanes(h)], kv_sem.at[i, h])

    def weights(k):
        return pltpu.make_async_copy(
            w_hbm.at[:, pl.ds(pl.multiple_of(k * width, width), width)], w_ref.at[k], w_sem.at[k]
        )

    load_q = pltpu.make_async_copy(q_hbm, q_ref, qg_sem.at[0])
    load_g = pltpu.make_async_copy(g_hbm, a_ref, qg_sem.at[1])
    for h in range(heads):
        load_head(0, h).start()
        load_head(1, h).start()
    load_q.start()
    load_g.start()

    barrier = pltpu.get_barrier_semaphore()
    for p in range(n_seq):
        @pl.when(p != at_seq)
        def _():
            pl.semaphore_signal(barrier, inc=1, device_id={"seq": p}, device_id_type=MESH)
    for peer in (sibling, above, below):
        pl.semaphore_signal(barrier, inc=1, device_id={"tp": peer}, device_id_type=MESH)

    def sums(h, carry):
        load_head(0, h).wait()
        load_head(1, h).wait()
        total = jnp.zeros((HD, HD), f32)
        for n, tokens in enumerate(blocks):
            u = k_ref[tokens, lanes(h)].astype(f32)
            ka = (u * sigmoid(u)).astype(bf16)
            k_ref[tokens, lanes(h)] = ka
            prefix[h, n] = total.astype(bf16)
            total += lax.dot_general(
                ka, v_ref[tokens, lanes(h)], (((0,), (0,)), ((), ())), preferred_element_type=f32
            )
        own_sum[h] = total.astype(bf16)
        return carry

    def state_copy(p, source, i):
        some = pl.ds(i * part, part)
        return pltpu.make_async_remote_copy(
            src_ref=own_sum.at[some], dst_ref=arrived.at[source, some],
            send_sem=send_sem.at[p, i], recv_sem=recv_sem.at[source, i],
            device_id={"seq": p}, device_id_type=MESH,
        )

    for i in range(2):
        lax.fori_loop(i * part, (i + 1) * part, sums, 0)
        if i == 0:
            pl.semaphore_wait(barrier, n_seq + 2)
        for p in range(n_seq - 1, -1, -1):
            @pl.when(p > at_seq)
            def _():
                state_copy(p, at_seq, i).start()

    for k in range(pieces):
        weights(k).start()
    load_q.wait()
    load_g.wait()

    causal = lax.broadcasted_iota(jnp.int32, (block, block), 0) >= lax.broadcasted_iota(
        jnp.int32, (block, block), 1
    )

    def within(h, carry):
        for n, tokens in enumerate(blocks):
            u = q_ref[tokens, lanes(h)].astype(f32)
            qa = (u * sigmoid(u)).astype(bf16)
            q_ref[tokens, lanes(h)] = qa
            scores = lax.dot_general(
                qa, k_ref[tokens, lanes(h)], (((1,), (1,)), ((), ())), preferred_element_type=f32
            )
            scores = jnp.where(causal, scores, 0.0).astype(bf16)
            out = jnp.dot(scores, v_ref[tokens, lanes(h)], preferred_element_type=f32)
            if n > 0:
                out += jnp.dot(qa, prefix[h, n], preferred_element_type=f32)
            local[tokens, lanes(h)] = out
        return carry

    lax.fori_loop(0, heads, within, 0)

    def outputs(h, carry):
        high = state[h].astype(bf16)
        low = (state[h] - high.astype(f32)).astype(bf16)
        gain = gain_ref[:, lanes(h)]
        for d in range(chips):
            tokens = slice(2 * d * rows, 2 * (d + 1) * rows)
            qa = q_ref[tokens, lanes(h)]
            out = local[tokens, lanes(h)] + jnp.dot(qa, high, preferred_element_type=f32)
            out += jnp.dot(qa, low, preferred_element_type=f32)
            scale = lax.rsqrt(jnp.mean(out * out, axis=-1, keepdims=True) + 1e-05)
            gate = sigmoid(a_ref[d, :, :, lanes(h)].reshape(2 * rows, HD).astype(f32))
            attn = (out * scale * gain * gate).astype(bf16)
            a_ref[d, :, :, lanes(h)] = attn.reshape(2, rows, HD)
        return carry

    state[...] = kv_ref[...]
    for i in range(2):
        some = slice(i * part, (i + 1) * part)
        for p in range(n_seq):
            @pl.when(p < at_seq)
            def _():
                state_copy(p, p, i).wait_recv()
                state[some] += arrived[p, some].astype(f32)
        lax.fori_loop(i * part, (i + 1) * part, outputs, 0)

    def pair_copy(k):
        return pltpu.make_async_remote_copy(
            src_ref=pair_out.at[k], dst_ref=pair_in.at[k],
            send_sem=pair_out_sem.at[k], recv_sem=pair_in_sem.at[k],
            device_id={"tp": sibling}, device_id_type=MESH,
        )

    def owner_above(t):
        return lax.rem(z + t, chips)

    def owner_below(t):
        return lax.rem(z + chips - t, chips)

    def up_copy(k, t):
        return pltpu.make_async_remote_copy(
            src_ref=own.at[k, owner_above(t)], dst_ref=from_low.at[k, t - 1],
            send_sem=up_sem.at[k, t - 1], recv_sem=low_sem.at[k, t - 1],
            device_id={"tp": above}, device_id_type=MESH,
        )

    def down_copy(k, t):
        return pltpu.make_async_remote_copy(
            src_ref=own.at[k, owner_below(t)], dst_ref=from_high.at[k, t - 1],
            send_sem=down_sem.at[k, t - 1], recv_sem=high_sem.at[k, t - 1],
            device_id={"tp": below}, device_id_type=MESH,
        )

    def partial(k, side):
        a = a_ref[:, side].reshape(chips * rows, depth)
        out = jnp.dot(a, w_ref[k], preferred_element_type=jnp.float32)
        return out.astype(own.dtype).reshape(chips, rows, width)

    def compute(k):
        weights(k).wait()
        pair_out[k] = partial(k, 1 - core)
        pair_copy(k).start()
        own[k] = partial(k, core)

    def chip_sum(k, d):
        return own[k, d].astype(jnp.float32) + pair_in[k, d].astype(jnp.float32)

    def begin(k, t, copy, owner):
        d = owner(t)
        own[k, d] = chip_sum(k, d).astype(own.dtype)
        copy(k, t).start()

    def relay(k, t, copy, owner, arrived):
        d = owner(t)
        copy(k, t + 1).wait_recv()
        total = chip_sum(k, d) + arrived[k, t].astype(jnp.float32)
        own[k, d] = total.astype(own.dtype)
        copy(k, t).start()

    def send_first(k):
        pair_copy(k).wait_recv()

        @pl.when(k % 2 == 0)
        def _():
            begin(k, half, up_copy, owner_above)
            begin(k, half - 1, down_copy, owner_below)

        @pl.when(k % 2 == 1)
        def _():
            begin(k, half, down_copy, owner_below)
            begin(k, half - 1, up_copy, owner_above)

    def send_on(k, t):
        if t < half - 1:
            relay(k, t, up_copy, owner_above, from_low)
            relay(k, t, down_copy, owner_below, from_high)
        else:
            @pl.when(k % 2 == 0)
            def _():
                relay(k, t, up_copy, owner_above, from_low)

            @pl.when(k % 2 == 1)
            def _():
                relay(k, t, down_copy, owner_below, from_high)

    def finish(k):
        up_copy(k, 1).wait_recv()
        down_copy(k, 1).wait_recv()
        total = chip_sum(k, z) + from_low[k, 0].astype(jnp.float32)
        total = total + from_high[k, 0].astype(jnp.float32)
        o_ref[:, pl.ds(pl.multiple_of(k * width, width), width)] = total.astype(o_ref.dtype)

    def sent(k):
        for t in range(half - 1, 0, -1):
            up_copy(k, t).wait_send()
            down_copy(k, t).wait_send()

        @pl.when(k % 2 == 0)
        def _():
            up_copy(k, half).wait_send()

        @pl.when(k % 2 == 1)
        def _():
            down_copy(k, half).wait_send()

    def step(k, carry):
        def at(lag, work):
            pl.when((k >= lag) & (k < pieces + lag))(lambda: work(k - lag))

        at(0, compute)
        at(half + 2, sent)
        at(1, send_first)
        for t in range(half - 1, 0, -1):
            at(1 + half - t, functools.partial(send_on, t=t))
        at(half + 1, finish)
        return carry

    lax.fori_loop(0, pieces + half + 2, step, 0)

    def drain(k, carry):
        pair_copy(k).wait_send()
        return carry

    lax.fori_loop(0, pieces, drain, 0)

    for p in range(n_seq):
        @pl.when(p > at_seq)
        def _():
            for i in range(2):
                state_copy(p, at_seq, i).wait_send()


def per_device(n_seq, n_tp, query, key_in, value, gate, kv_start, norm_gain, w_out):
    tokens, depth = query.shape
    columns = w_out.shape[1]
    heads = depth // HD
    rows = tokens // n_tp
    chips = n_tp // 2
    block = min(256, tokens)
    width = 256
    pieces = columns // width
    bf16, f32 = jnp.bfloat16, jnp.float32
    vmem = pl.BlockSpec(memory_space=pltpu.VMEM)
    hbm = pl.BlockSpec(memory_space=pl.ANY)
    chunk = lambda n: pltpu.VMEM((pieces, n, rows, width), bf16)
    dma = lambda *n: pltpu.SemaphoreType.DMA(n)
    return pl.pallas_call(
        functools.partial(layer_kernel, n_seq, chips, block),
        out_shape=jax.ShapeDtypeStruct((rows, columns), bf16),
        in_specs=[hbm, hbm, hbm, hbm, vmem, vmem, hbm],
        out_specs=vmem,
        scratch_shapes=[
            pltpu.VMEM((tokens, depth), bf16),
            pltpu.VMEM((tokens, depth), bf16),
            pltpu.VMEM((tokens, depth), bf16),
            pltpu.VMEM((chips, 2, rows, depth), bf16),
            pltpu.VMEM((tokens, depth), f32),
            pltpu.VMEM((heads, tokens // block, HD, HD), bf16),
            pltpu.VMEM((heads, HD, HD), f32),
            pltpu.VMEM((heads, HD, HD), bf16),
            pltpu.VMEM((n_seq, heads, HD, HD), bf16),
            pltpu.VMEM((pieces, depth, width), bf16),
            chunk(chips), chunk(chips), chunk(chips), chunk(chips // 2), chunk(chips // 2),
            dma(2), dma(2, heads), dma(n_seq, 2), dma(n_seq, 2),
            dma(pieces), dma(pieces), dma(pieces),
            dma(pieces, chips // 2), dma(pieces, chips // 2),
            dma(pieces, chips // 2), dma(pieces, chips // 2),
        ],
        compiler_params=pltpu.CompilerParams(
            collective_id=0, has_side_effects=True, vmem_limit_bytes=62 * 2**20
        ),
        cost_estimate=pl.CostEstimate(
            flops=2 * tokens * depth * (columns + 4 * block),
            bytes_accessed=2 * depth * (columns + 4 * tokens),
            transcendentals=3 * tokens * depth,
        ),
    )(
        query, key_in, value, gate.reshape(chips, 2, rows, depth), kv_start,
        norm_gain.reshape(1, depth), w_out,
    )


def solution(mesh):
    in_specs = (
        P("seq", "tp"),
        P("seq", "tp"),
        P("seq", "tp"),
        P("seq", "tp"),
        P("tp", None, None),
        P("tp"),
        P("tp", None),
    )
    out_specs = P(("seq", "tp"), None)
    return jax.shard_map(
        functools.partial(per_device, mesh.shape["seq"], mesh.shape["tp"]), mesh=mesh, in_specs=in_specs, out_specs=out_specs, check_vma=False
    )
```

time: 203 us -> 134 us (0.66)
  matrix products: 33.8 us -> 0 us
  local copies, waits for them, and re-layouts: 18.2 us -> 2.69 us
  between operations: 13.5 us -> 0.01 us
  other arithmetic: 13 us -> 0 us
  Pallas kernels: 123 us -> 131 us
    dot_general x4 -> x0, matrix products: 33.8 us -> none  [the longest x1 18.3 us: per_device(): jnp.einsum('nhts,nshe->nthe', scores, va.astype(jnp.float32), precision=h...]
    pallas_call x1, Pallas kernels: 123 us -> 131 us  [per_device(): pl.pallas_call(functools.partial(layer_kernel, n_seq, chips, block), out_...]
    unnamed x2 -> x0, other arithmetic: 5.66 us -> none
    unnamed x20 -> x1, local copies, waits for them, and re-layouts: 8.26 us -> 2.69 us
    add x1 -> x0, local copies, waits for them, and re-layouts: 5.4 us -> none  [per_device(): heads_out = (inter + intra).reshape(rows, heads, HD)]
    convert_element_type x2 -> x0, other arithmetic: 3.72 us -> none  [the longest x1 3.71 us: per_device(): (normed * norm_gain[None, :] * jax.nn.sigmoid(gate.astype(jnp.float32)))....]
    reshape x1 -> x0, local copies, waits for them, and re-layouts: 3.17 us -> none  [per_device(): va = value.reshape(count, block, heads, HD)]
  transfers between devices with their start and end apart: 1 -> 0, of which waited for: 0 -> 0; matrix products, arithmetic and copies ran while one was open for 15% -> 0% of each run, Pallas kernels for 0% -> 0%
where the time goes in v5:
time: 134 us
  Pallas kernels  131 us (98%)
  local copies, waits for them, and re-layouts  2.69 us (2%)
    pallas_call x1, Pallas kernels, per_device(): pl.pallas_call(functools.partial(layer_kernel, n_seq, chips, block), out_...  131 us
    unnamed x1, local copies, waits for them, and re-layouts  2.69 us

profile of v5, /device:TPU:6, one launch (start us, length us, event | category | flops | bytes accessed | tf_op | source)
XLA Modules:
  0.0 133.7 jit_solution(18218120753580577005)
XLA Ops:
  0.0 131.0 %shard_map.73 = bf16[128,6144]{1,0:T(8,128)(2,1)} custom-call(bf16[1024,1024]{1,0:T(8,128)(2,1)} %q_hbm.1, bf16[1024,1024]{1,0:T(8,128)(2,1)} %k_hbm.1, bf16[1024,1024]{1,0:T(8,128)(2,1)} %v_hbm.1, bf16[4,2,128,1024]{3,2,1,0:T(8,128)(2,1)} %bitcast.2, f32[8,128,128]{2,1,0:T(8,128)} %kv_ref.1, f32[1,1024]{1,0:T(1,128)} %bitcast.3, bf16[1024,6144]{1,0:T(8,128)(2,1)} %w_hbm.1), custom_call_target="tpu_custom_call" | custom-call | flops 15032385536 | bytes 20971520 | tf_op jit(solution)/shard_map/pallas_call | solution.py:290
  131.0 2.7 %copy.9 = bf16[128,6144]{1,0:T(8,128)(2,1)} copy(bf16[128,6144]{1,0:T(8,128)(2,1)} %shard_map.73) | data formatting | bytes 3145728

commit v6 on v5

--- a/solution.py
+++ b/solution.py
@@ -32,9 +32,8 @@
     me = lax.axis_index("tp")
     z, core = me // 2, me % 2
     sibling = me + 1 - 2 * core
-    above = lax.rem(z + 1, chips) * 2 + core
-    below = lax.rem(z + chips - 1, chips) * 2 + core
-    half = chips // 2
+    top = chips - 1
+    ahead = 3
 
     def lanes(h):
         return pl.ds(pl.multiple_of(h * HD, HD), HD)
@@ -61,8 +60,16 @@
         @pl.when(p != at_seq)
         def _():
             pl.semaphore_signal(barrier, inc=1, device_id={"seq": p}, device_id_type=MESH)
-    for peer in (sibling, above, below):
-        pl.semaphore_signal(barrier, inc=1, device_id={"tp": peer}, device_id_type=MESH)
+    pl.semaphore_signal(barrier, inc=1, device_id={"tp": sibling}, device_id_type=MESH)
+
+    @pl.when(z > 0)
+    def _():
+        pl.semaphore_signal(barrier, inc=1, device_id={"tp": me - 2}, device_id_type=MESH)
+
+    @pl.when(z < top)
+    def _():
+        pl.semaphore_signal(barrier, inc=1, device_id={"tp": me + 2}, device_id_type=MESH)
+
 
     def sums(h, carry):
         load_head(0, h).wait()
@@ -90,7 +97,7 @@
     for i in range(2):
         lax.fori_loop(i * part, (i + 1) * part, sums, 0)
         if i == 0:
-            pl.semaphore_wait(barrier, n_seq + 2)
+            pl.semaphore_wait(barrier, n_seq + jnp.minimum(z, 1) + jnp.minimum(top - z, 1))
         for p in range(n_seq - 1, -1, -1):
             @pl.when(p > at_seq)
             def _():
@@ -154,24 +161,18 @@
             device_id={"tp": sibling}, device_id_type=MESH,
         )
 
-    def owner_above(t):
-        return lax.rem(z + t, chips)
-
-    def owner_below(t):
-        return lax.rem(z + chips - t, chips)
-
-    def up_copy(k, t):
+    def up_copy(k, j):
         return pltpu.make_async_remote_copy(
-            src_ref=own.at[k, owner_above(t)], dst_ref=from_low.at[k, t - 1],
-            send_sem=up_sem.at[k, t - 1], recv_sem=low_sem.at[k, t - 1],
-            device_id={"tp": above}, device_id_type=MESH,
-        )
-
-    def down_copy(k, t):
+            src_ref=own.at[k, top - j], dst_ref=from_low.at[k, j],
+            send_sem=up_sem.at[k, j], recv_sem=low_sem.at[k, j],
+            device_id={"tp": me + 2}, device_id_type=MESH,
+        )
+
+    def down_copy(k, j):
         return pltpu.make_async_remote_copy(
-            src_ref=own.at[k, owner_below(t)], dst_ref=from_high.at[k, t - 1],
-            send_sem=down_sem.at[k, t - 1], recv_sem=high_sem.at[k, t - 1],
-            device_id={"tp": below}, device_id_type=MESH,
+            src_ref=own.at[k, j], dst_ref=from_high.at[k, j],
+            send_sem=down_sem.at[k, j], recv_sem=high_sem.at[k, j],
+            device_id={"tp": me - 2}, device_id_type=MESH,
         )
 
     def partial(k, side):
@@ -188,77 +189,69 @@
     def chip_sum(k, d):
         return own[k, d].astype(jnp.float32) + pair_in[k, d].astype(jnp.float32)
 
-    def begin(k, t, copy, owner):
-        d = owner(t)
-        own[k, d] = chip_sum(k, d).astype(own.dtype)
-        copy(k, t).start()
-
-    def relay(k, t, copy, owner, arrived):
-        d = owner(t)
-        copy(k, t + 1).wait_recv()
-        total = chip_sum(k, d) + arrived[k, t].astype(jnp.float32)
-        own[k, d] = total.astype(own.dtype)
-        copy(k, t).start()
-
-    def send_first(k):
-        pair_copy(k).wait_recv()
-
-        @pl.when(k % 2 == 0)
-        def _():
-            begin(k, half, up_copy, owner_above)
-            begin(k, half - 1, down_copy, owner_below)
-
-        @pl.when(k % 2 == 1)
-        def _():
-            begin(k, half, down_copy, owner_below)
-            begin(k, half - 1, up_copy, owner_above)
-
-    def send_on(k, t):
-        if t < half - 1:
-            relay(k, t, up_copy, owner_above, from_low)
-            relay(k, t, down_copy, owner_below, from_high)
-        else:
-            @pl.when(k % 2 == 0)
-            def _():
-                relay(k, t, up_copy, owner_above, from_low)
-
-            @pl.when(k % 2 == 1)
-            def _():
-                relay(k, t, down_copy, owner_below, from_high)
+    def send(k, j, d, copy, arrived_there, inner):
+        @pl.when(inner)
+        def _():
+            copy(k, j).wait_recv()
+            total = chip_sum(k, d) + arrived_there[k, j].astype(f32)
+            own[k, d] = total.astype(own.dtype)
+
+        @pl.when(jnp.logical_not(inner))
+        def _():
+            own[k, d] = chip_sum(k, d).astype(own.dtype)
+
+        @pl.when(k >= ahead)
+        def _():
+            copy(k - ahead, j).wait_send()
+
+        copy(k, j).start()
+
+    def send_up(k):
+        for j in range(top):
+            pl.when(top - j > z)(lambda: send(k, j, top - j, up_copy, from_low, z > 0))
+
+    def send_down(k):
+        for j in range(top):
+            pl.when(j < z)(lambda: send(k, j, j, down_copy, from_high, z < top))
 
     def finish(k):
-        up_copy(k, 1).wait_recv()
-        down_copy(k, 1).wait_recv()
-        total = chip_sum(k, z) + from_low[k, 0].astype(jnp.float32)
-        total = total + from_high[k, 0].astype(jnp.float32)
-        o_ref[:, pl.ds(pl.multiple_of(k * width, width), width)] = total.astype(o_ref.dtype)
-
-    def sent(k):
-        for t in range(half - 1, 0, -1):
-            up_copy(k, t).wait_send()
-            down_copy(k, t).wait_send()
-
-        @pl.when(k % 2 == 0)
-        def _():
-            up_copy(k, half).wait_send()
-
-        @pl.when(k % 2 == 1)
-        def _():
-            down_copy(k, half).wait_send()
+        out = pl.ds(pl.multiple_of(k * width, width), width)
+        total = chip_sum(k, z)
+
+        @pl.when(z == 0)
+        def _():
+            down_copy(k, z).wait_recv()
+            o_ref[:, out] = (total + from_high[k, 0].astype(f32)).astype(o_ref.dtype)
+
+        @pl.when(z == top)
+        def _():
+            up_copy(k, 0).wait_recv()
+            o_ref[:, out] = (total + from_low[k, 0].astype(f32)).astype(o_ref.dtype)
+
+        @pl.when((z > 0) & (z < top))
+        def _():
+            up_copy(k, top - z).wait_recv()
+            down_copy(k, z).wait_recv()
+            both = from_low[k, top - z].astype(f32) + from_high[k, z].astype(f32)
+            o_ref[:, out] = (total + both).astype(o_ref.dtype)
 
     def step(k, carry):
         def at(lag, work):
             pl.when((k >= lag) & (k < pieces + lag))(lambda: work(k - lag))
 
         at(0, compute)
-        at(half + 2, sent)
-        at(1, send_first)
-        for t in range(half - 1, 0, -1):
-            at(1 + half - t, functools.partial(send_on, t=t))
-        at(half + 1, finish)
-        return carry
-
-    lax.fori_loop(0, pieces + half + 2, step, 0)
+        at(1, lambda i: pair_copy(i).wait_recv())
+        at(1 + z, send_up)
+        at(1 + top - z, send_down)
+        at(1 + top, finish)
+        return carry
+
+    lax.fori_loop(0, pieces + top + 1, step, 0)
+
+    for k in range(pieces - ahead, pieces):
+        for j in range(top):
+            pl.when(top - j > z)(lambda: up_copy(k, j).wait_send())
+            pl.when(j < z)(lambda: down_copy(k, j).wait_send())
 
     def drain(k, carry):
         pair_copy(k).wait_send()
@@ -303,11 +296,11 @@
             pltpu.VMEM((heads, HD, HD), bf16),
             pltpu.VMEM((n_seq, heads, HD, HD), bf16),
             pltpu.VMEM((pieces, depth, width), bf16),
-            chunk(chips), chunk(chips), chunk(chips), chunk(chips // 2), chunk(chips // 2),
+            chunk(chips), chunk(chips), chunk(chips), chunk(chips - 1), chunk(chips - 1),
             dma(2), dma(2, heads), dma(n_seq, 2), dma(n_seq, 2),
             dma(pieces), dma(pieces), dma(pieces),
-            dma(pieces, chips // 2), dma(pieces, chips // 2),
-            dma(pieces, chips // 2), dma(pieces, chips // 2),
+            dma(pieces, chips - 1), dma(pieces, chips - 1),
+            dma(pieces, chips - 1), dma(pieces, chips - 1),
         ],
         compiler_params=pltpu.CompilerParams(
             collective_id=0, has_side_effects=True, vmem_limit_bytes=62 * 2**20

time: 134 us -> 138 us (1.030)
  Pallas kernels: 131 us -> 135 us
    pallas_call x1, Pallas kernels: 131 us -> 135 us  [per_device(): pl.pallas_call(functools.partial(layer_kernel, n_seq, chips, block), out_...]
where the time goes in v6:
time: 138 us
  Pallas kernels  135 us (98%)
  local copies, waits for them, and re-layouts  2.69 us (2%)
    pallas_call x1, Pallas kernels, per_device(): pl.pallas_call(functools.partial(layer_kernel, n_seq, chips, block), out_...  135 us

profile of v6, /device:TPU:6, one launch (start us, length us, event | category | flops | bytes accessed | tf_op | source)
XLA Modules:
  0.0 137.6 jit_solution(9561483344027745785)
XLA Ops:
  0.0 134.9 %shard_map.73 = bf16[128,6144]{1,0:T(8,128)(2,1)} custom-call(bf16[1024,1024]{1,0:T(8,128)(2,1)} %q_hbm.1, bf16[1024,1024]{1,0:T(8,128)(2,1)} %k_hbm.1, bf16[1024,1024]{1,0:T(8,128)(2,1)} %v_hbm.1, bf16[4,2,128,1024]{3,2,1,0:T(8,128)(2,1)} %bitcast.2, f32[8,128,128]{2,1,0:T(8,128)} %kv_ref.1, f32[1,1024]{1,0:T(1,128)} %bitcast.3, bf16[1024,6144]{1,0:T(8,128)(2,1)} %w_hbm.1), custom_call_target="tpu_custom_call" | custom-call | flops 15032385536 | bytes 20971520 | tf_op jit(solution)/shard_map/pallas_call | solution.py:283
  134.9 2.7 %copy.9 = bf16[128,6144]{1,0:T(8,128)(2,1)} copy(bf16[128,6144]{1,0:T(8,128)(2,1)} %shard_map.73) | data formatting | bytes 3145728
